TPU v7x, 1024 devices: a whole 4x4x32 slice. The times are simulated.
1024 devices in a mesh: node: 32 (over z), local: 8 (over x, core), cuts: 4 (over y).
Axes of the slice: x: 4, y: 4, z: 32, core: 2. Of those that a mesh axis runs over, the one named last changes fastest.
Arguments:
- tokens: bfloat16 [4096, 2048], P('node'), may hold values from -6 to 6
- expert_ids: int32 [4096, 8], P('node'), may hold values from 0 to 127, as said below
- route_weight: float32 [4096, 8], P('node'), may hold values from 0.25 to 1
- gate_weight: bfloat16 [128, 2048, 1536], P(('node', 'cuts'), None, 'local'), may hold values from -0.125 to 0.125
- up_weight: bfloat16 [128, 2048, 1536], P(('node', 'cuts'), None, 'local'), may hold values from -0.125 to 0.125
- down_weight: bfloat16 [128, 1536, 2048], P(('node', 'cuts'), 'local'), may hold values from -0.15625 to 0.15625
Outputs:
- mixed: bfloat16 [4096, 2048], P('node', ('local', 'cuts'))
Inputs may be any that keep to these rules, and one draw needn't show every extreme that they name: `expert_ids`: each token names 8 different experts, lying in at most 4 groups (expert e belongs to group e // 4). In each aligned block of 128 tokens no expert and no group is named by more than 16 tokens, and some expert by exactly 16.
All inputs are finite; a program needn't handle non-finite values.
Results may differ from a plain program's by a relative error of at most 0.02.
Values may be sent and summed in bfloat16 or wider, within the bound.
No kernel may reach another device: no remote copies, remote signals or barrier semaphores. Data moves between devices by JAX's collectives and lax.ppermute only.
A program may use at most 32 MiB of HBM per device.

v0:
```python
import jax
import jax.numpy as jnp
from jax import lax
from jax.sharding import PartitionSpec as P


def combine(values, owners, weights, tok_rows):
    features = values.shape[-1]
    scaled = values.astype(jnp.float32) * weights[..., None]
    return jax.ops.segment_sum(
        scaled.reshape(-1, features), owners.reshape(-1), num_segments=tok_rows
    )


def per_device(tokens, expert_ids, route_weight, gate_weight, up_weight, down_weight):
    node_count = lax.axis_size("node")
    group_width = lax.axis_size("cuts")
    column = lax.axis_index("cuts")
    tok_rows, features = tokens.shape
    capacity = tok_rows * 4 // node_count
    targets = lax.broadcasted_iota(jnp.int32, (1, 1, node_count), 2) * group_width + column
    matches = expert_ids[:, :, None] == targets
    visits = jnp.any(matches, axis=1).astype(jnp.int32)
    weights = jnp.sum(jnp.where(matches, route_weight[:, :, None], 0.0), axis=1)
    seat_rank = jnp.cumsum(visits, axis=0) - visits
    places = lax.broadcasted_iota(jnp.int32, (1, 1, capacity), 2)
    seated = (seat_rank[:, :, None] == places) & (visits[:, :, None] > 0)
    seated_int = seated.astype(jnp.int32)
    row_order = lax.broadcasted_iota(jnp.int32, (tok_rows, 1, 1), 0)
    slot_token = jnp.sum(seated_int * row_order, axis=0)
    slot_live = jnp.sum(seated_int, axis=0)
    slot_weight = jnp.sum(jnp.where(seated, weights[:, :, None], 0.0), axis=0)
    outgoing = jnp.where(
        slot_live[:, :, None] > 0, jnp.take(tokens, slot_token, axis=0), jnp.zeros((), tokens.dtype)
    )
    row_block = lax.all_to_all(outgoing, "node", split_axis=0, concat_axis=0, tiled=True)
    flat_rows = row_block.reshape(-1, features)
    gate_value = jnp.dot(flat_rows, gate_weight[0], preferred_element_type=jnp.float32)
    up_value = jnp.dot(flat_rows, up_weight[0], preferred_element_type=jnp.float32)
    hidden = (jax.nn.silu(gate_value) * up_value).astype(jnp.bfloat16)
    partial_value = jnp.dot(hidden, down_weight[0], preferred_element_type=jnp.float32).astype(
        jnp.bfloat16
    )
    answers = lax.all_to_all(
        partial_value.reshape(row_block.shape), "node", split_axis=0, concat_axis=0, tiled=True
    )
    partial_out = combine(answers, slot_token, slot_weight, tok_rows)
    totals = lax.psum_scatter(
        partial_out.astype(jnp.bfloat16), ("local", "cuts"), scatter_dimension=1, tiled=True
    )
    return totals


def solution(mesh):
    in_specs = (
        P("node", None),
        P("node", None),
        P("node", None),
        P(("node", "cuts"), None, "local"),
        P(("node", "cuts"), None, "local"),
        P(("node", "cuts"), "local", None),
    )
    out_specs = P("node", ("local", "cuts"))
    return jax.shard_map(
        per_device, mesh=mesh, in_specs=in_specs, out_specs=out_specs, check_vma=False
    )
```

profile of v0, /device:TPU:1, one launch (start us, length us, event | category | flops | bytes accessed | tf_op | source)
XLA Modules:
  0.0 578.6 jit_solution(16938666660789169381)
XLA Ops:
  6.5 0.9 compare_reduce_fusion
  7.4 0.1 copy.16
  7.6 0.1 copy.18
  7.7 0.2 reduce_window_sum.11
  7.8 0.1 copy.17
  7.9 1.2 convert_reduce_fusion
  9.1 0.1 reshape.63
  9.2 2.5 gather_fusion
  11.7 0.3 select_select_fusion
  12.0 224.2 %all_to_all.10 = bf16[32,16,2048]{2,1,0:T(8,128)(2,1)S(1)} all-to-all(bf16[32,16,2048]{2,1,0:T(8,128)(2,1)S(1)} %select_select_fusion), channel_id=1, replica_groups=mesh['node'=32,'local'=8,'cuts'=4] {'node'}, dimensions={0} | all-to-all | bytes 4194304 | tf_op jit(solution)/shard_map/all_to_all | solution.py:36
  236.2 0.8 fusion.4
  237.0 4.1 convolution_convert_fusion
  241.1 7.7 %all-to-all-start.1 = ((bf16[32,16,2048]{2,1,0:T(8,128)(2,1)}), bf16[32,16,2048]{2,1,0:T(8,128)(2,1)S(1)}, u32[]{:S(2)}, u32[]{:S(2)}) async-start(bf16[32,16,2048]{2,1,0:T(8,128)(2,1)} %bitcast.24), calls=%async_computation.1 | async-start | bytes 4194304 | tf_op jit(solution)/shard_map/all_to_all | solution.py:44
  248.8 0.2 reduce-scatter.4.cloned.1.call-start
  249.1 0.1 reshape.71
  249.1 0.1 fusion.15
  249.2 0.1 select_reduce_fusion
  249.4 191.6 %all-to-all-done.1 = bf16[32,16,2048]{2,1,0:T(8,128)(2,1)S(1)} async-done(((bf16[32,16,2048]{2,1,0:T(8,128)(2,1)}), bf16[32,16,2048]{2,1,0:T(8,128)(2,1)S(1)}, u32[]{:S(2)}, u32[]{:S(2)}) %all-to-all-start.1) | async-done | bytes 2097184 | tf_op jit(solution)/shard_map/all_to_all | solution.py:44
  441.0 2.3 convert_multiply_fusion
  443.3 8.7 %scatter_custom_fusion = f32[128,2048]{1,0:T(8,128)S(1)} fusion(s32[512]{0:T(512)S(1)} %reshape.71, f32[512,2048]{1,0:T(8,128)} %bitcast.23, f32[]{:T(128)} %constant.12.clone.1), kind=kCustom, calls=%fused_computation.11 | custom fusion | flops 1048576 | bytes 1049088 | tf_op jit(solution)/shard_map/scatter-add | solution.py:10
  452.0 0.1 convert_element_type.34
  452.1 1.0 copy.20
  453.1 0.0 reduce-scatter.4.cloned.1.call-update
  453.1 118.7 %reduce-scatter.4.cloned.1.call-done = bf16[64,128]{1,0:T(8,128)(2,1)} async-done(((bf16[2048,128]{1,0:T(8,128)(2,1)}), bf16[64,128]{1,0:T(8,128)(2,1)}) %reduce-scatter.4.cloned.1.call-update) | async-done | bytes 16400
  (16 shorter events, 0.1 us)
Async XLA Ops:
  6.5 230.5 %copy-start = (bf16[1,192,2048]{2,1,0:T(8,128)(2,1)S(1)}, bf16[1,192,2048]{2,1,0:T(8,128)(2,1)}, u32[]{:S(2)}) copy-start(bf16[1,192,2048]{2,1,0:T(8,128)(2,1)} %param.11) | copy-start | bytes 2359300
  6.5 2.7 copy-start.1
  12.0 224.2 %copy-start.4 = (bf16[1,2048,192]{1,2,0:T(8,128)(2,1)S(1)}, bf16[1,2048,192]{1,2,0:T(8,128)(2,1)}, u32[]{:S(2)}) copy-start(bf16[1,2048,192]{1,2,0:T(8,128)(2,1)} %param.9) | copy-start | bytes 2359300
  241.1 8.0 %copy-start.2 = (s32[128,8]{0,1:T(8,128)S(1)}, s32[128,8]{0,1:T(8,128)}, u32[]{:S(2)}) copy-start(s32[128,8]{0,1:T(8,128)} %param.7) | copy-start | bytes 12292
  241.1 8.0 %copy-start.3 = (f32[128,8]{0,1:T(8,128)S(1)}, f32[128,8]{0,1:T(8,128)}, u32[]{:S(2)}) copy-start(f32[128,8]{0,1:T(8,128)} %param.8) | copy-start | bytes 12292
  241.1 199.9 %all-to-all-start.1 = ((bf16[32,16,2048]{2,1,0:T(8,128)(2,1)}), bf16[32,16,2048]{2,1,0:T(8,128)(2,1)S(1)}, u32[]{:S(2)}, u32[]{:S(2)}) async-start(bf16[32,16,2048]{2,1,0:T(8,128)(2,1)} %bitcast.24), calls=%async_computation.1 | async-start | bytes 4194304 | tf_op jit(solution)/shard_map/all_to_all | solution.py:44
  248.8 323.0 %reduce-scatter.4.cloned.1.call-start = ((), (), s32[]{:S(2)}) async-start(), calls=%async_computation.3 | async-start | bytes 540672
Sparse Core Ops, SparseCore 0:
  453.2 118.5 reduce-scatter.3
where the time goes:
time: 580 us; the launch traced here: 579 us
  waiting for transfers between devices  310 us (53%)
  blocking collectives  224 us (39%)
  other arithmetic  13.9 us (2%)
  between operations  13.5 us (2%)
  starting transfers between devices  7.92 us (1%)
    all_to_all x1, blocking collectives, per_device(): lax.all_to_all(outgoing, 'node', split_axis=0, concat_axis=0, tiled=True)  224 us
    all_to_all x1, waiting for transfers between devices, per_device(): lax.all_to_all(partial_value.reshape(row_block.shape), 'node', split_axis...  192 us
    unnamed x2, waiting for transfers between devices  119 us
  transfers between devices with their start and end apart: 2, of which 2 were waited for; matrix products, arithmetic and copies ran while one was open for 0% of the time, Pallas kernels for 0%

commit v1 on v0

v1 whole, which is shorter than its diff:
```python
import functools

import jax
import jax.numpy as jnp
from jax import lax
from jax.experimental import pallas as pl
from jax.experimental.pallas import tpu as pltpu
from jax.sharding import Mesh, PartitionSpec as P

F32 = jnp.float32
BF16 = jnp.bfloat16
NODES = 32
CHIPS = 16
HALF = 8
LANES = 128
WIDTH = 2048
FF = 192
ROWS = NODES * HALF

VMEM = pl.BlockSpec(memory_space=pltpu.VMEM)
SMEM = pl.BlockSpec(memory_space=pltpu.SMEM)
PARAMS = pltpu.CompilerParams(vmem_limit_bytes=40 * 1024 * 1024)


def seat_kernel(where_ref, ids_ref, route_ref, tok_ref, out_ref, pos_ref):
    core = where_ref[0]
    column = where_ref[1]
    tokens = tok_ref.shape[0]
    groups = lax.broadcasted_iota(jnp.int32, (NODES, tokens), 0)
    named = jnp.zeros((NODES, tokens), F32)
    weight = jnp.zeros((NODES, tokens), F32)
    for k in range(ids_ref.shape[0]):
        ids = ids_ref[k : k + 1, :]
        hit = (ids >> 2) == groups
        named = jnp.where(hit, 1.0, named)
        weight = weight + jnp.where(hit & ((ids & 3) == column), route_ref[k : k + 1, :], 0.0)
    before = lax.broadcasted_iota(jnp.int32, (tokens, tokens), 0) < lax.broadcasted_iota(
        jnp.int32, (tokens, tokens), 1
    )
    rank = jnp.dot(named.astype(BF16), before.astype(F32).astype(BF16), preferred_element_type=F32)
    pos = jnp.where(named > 0.0, rank, -1.0)
    pos_ref[...] = pos
    slot = lax.broadcasted_iota(jnp.int32, (1, HALF, 1), 1) + core * HALF
    seated = pos[:, None, :] == slot.astype(F32)
    rows = jnp.where(seated, 1.0, 0.0).reshape(ROWS, tokens).astype(BF16)
    picked = jnp.dot(rows, tok_ref[...], preferred_element_type=F32)
    scale = jnp.sum(jnp.where(seated, weight[:, None, :], 0.0), axis=2, keepdims=True)
    high = scale.astype(BF16).astype(F32)
    lane = lax.broadcasted_iota(jnp.int32, (1, 1, LANES), 2)
    scale = jnp.where(lane < 64, high, scale - high)
    out_ref[:, 0:HALF, :] = picked.reshape(NODES, HALF, LANES).astype(BF16)
    out_ref[:, HALF : 2 * HALF, :] = scale.astype(BF16)


def expert_kernel(x_ref, scale_ref, own_ref, other_ref, out_ref):
    x = jnp.concatenate([x_ref[q] for q in range(CHIPS)], axis=1)
    scale = scale_ref[:, HALF : 2 * HALF, :].reshape(ROWS, LANES).astype(F32)
    scale = scale[:, 0:1] + scale[:, 64:65]
    hidden = []
    for w_ref in (own_ref, other_ref):
        gate = lax.dot_general(
            x, w_ref[0:FF, :], (((1,), (1,)), ((), ())), preferred_element_type=F32
        )
        up = lax.dot_general(
            x, w_ref[FF : 2 * FF, :], (((1,), (1,)), ((), ())), preferred_element_type=F32
        )
        hidden.append((gate / (1.0 + jnp.exp(-gate)) * up).astype(BF16))
    low = lax.broadcasted_iota(jnp.int32, (ROWS, LANES), 1) < 64
    for i in range(4):
        part = 0.0
        for h, w_ref in zip(hidden, (own_ref, other_ref)):
            part = part + jnp.dot(
                h, w_ref[2 * FF : 3 * FF, i * 512 : (i + 1) * 512], preferred_element_type=F32
            )
        part = part * scale
        for b in range(2):
            one = part[:, b * LANES : (b + 1) * LANES]
            two = part[:, (b + 2) * LANES : (b + 3) * LANES]
            mixed = pltpu.roll(jnp.where(low, two, one), 64, 1)
            out_ref[4 * i + 2 * b] = jnp.where(low, one, mixed).astype(BF16)
            out_ref[4 * i + 2 * b + 1] = jnp.where(low, mixed, two).astype(BF16)


def sum_kernel(in_ref, out_ref):
    total = in_ref[0].astype(F32)
    for q in range(1, CHIPS):
        total = total + in_ref[q].astype(F32)
    total = total.reshape(NODES, HALF, LANES)
    turned = pltpu.roll(pltpu.roll(total, 64, 2), 4, 1)
    row = lax.broadcasted_iota(jnp.int32, (NODES, HALF, LANES), 1)
    lane = lax.broadcasted_iota(jnp.int32, (NODES, HALF, LANES), 2)
    out_ref[...] = jnp.where((row < 4) == (lane < 64), total, turned).astype(BF16)


def mix_kernel(in_ref, pos_ref, out_ref):
    tokens = pos_ref.shape[1]
    pos = pos_ref[...]
    row = lax.broadcasted_iota(jnp.int32, (1, HALF, 1), 1)
    values = in_ref[...]
    parts = []
    for h in range(2):
        slot = (row >> 2) * HALF + h * 4 + (row & 3)
        seated = jnp.where(pos[:, None, :] == slot.astype(F32), 1.0, 0.0)
        seated = seated.reshape(ROWS, tokens).astype(BF16)
        parts.append(
            lax.dot_general(
                values, seated, (((0,), (0,)), ((), ())), preferred_element_type=F32
            )
        )
    out_ref[...] = (parts[0][0:64] + parts[1][64:128]).astype(BF16)


def call(kernel, outs, *args, specs=None):
    shapes = [jax.ShapeDtypeStruct(s, d) for s, d in outs]
    many = len(shapes) > 1
    return pl.pallas_call(
        kernel,
        out_shape=shapes if many else shapes[0],
        in_specs=specs or [VMEM] * len(args),
        out_specs=[VMEM] * len(shapes) if many else VMEM,
        compiler_params=PARAMS,
    )(*args)


def per_device(tokens, expert_ids, route_weight, gate_weight, up_weight, down_weight):
    x, core, column = lax.axis_index("x"), lax.axis_index("core"), lax.axis_index("cuts")
    exchange = functools.partial(lax.all_to_all, split_axis=0, concat_axis=0, tiled=True)
    own = jnp.concatenate([gate_weight[0].T, up_weight[0].T, down_weight[0]], axis=0)
    other = lax.ppermute(own, "core", [(0, 1), (1, 0)])

    chip = x * 4 + column
    block = lax.dynamic_slice_in_dim(tokens, chip * LANES, LANES, axis=1)
    where = jnp.stack([core, column]).astype(jnp.int32)
    seats, pos = call(
        seat_kernel,
        [((NODES, 2 * HALF, LANES), BF16), ((NODES, tokens.shape[0]), F32)],
        where,
        expert_ids.T,
        route_weight.T,
        block,
        specs=[SMEM, VMEM, VMEM, VMEM],
    )
    seats = exchange(seats, "node")
    mine = seats[:, :HALF].reshape(1, ROWS, LANES)
    rows = exchange(jnp.broadcast_to(mine, (CHIPS, ROWS, LANES)), ("x", "cuts"))
    parts = call(expert_kernel, [((CHIPS, ROWS, LANES), BF16)], rows, seats, own, other)
    parts = exchange(parts, ("x", "cuts"))
    total = call(sum_kernel, [((NODES, HALF, LANES), BF16)], parts)
    answers = exchange(total.reshape(2 * NODES, HALF // 2, LANES), ("node", "core"))
    mixed = call(mix_kernel, [((64, tokens.shape[0]), BF16)], answers.reshape(ROWS, LANES), pos)
    return mixed.T


def solution(mesh):
    fine = Mesh(mesh.devices.reshape(NODES, 4, 2, 4), ("node", "x", "core", "cuts"))
    in_specs = (
        P("node", None),
        P("node", None),
        P("node", None),
        P(("node", "cuts"), None, ("x", "core")),
        P(("node", "cuts"), None, ("x", "core")),
        P(("node", "cuts"), ("x", "core"), None),
    )
    out_specs = P("node", ("x", "core", "cuts"))
    return jax.shard_map(
        per_device, mesh=fine, in_specs=in_specs, out_specs=out_specs, check_vma=False
    )
```

time: 580 us -> 143 us (0.25)
  waiting for transfers between devices: 310 us -> 0.01 us
  blocking collectives: 224 us -> 119 us
  between operations: 13.5 us -> 0.07 us
  other arithmetic: 13.9 us -> 1.9 us
  starting transfers between devices: 7.92 us -> 16.1 us
    all_to_all x1 -> x0, waiting for transfers between devices: 192 us -> none  [per_device(): lax.all_to_all(partial_value.reshape(row_block.shape), 'node', split_axis...]
    unnamed x2 -> x0, waiting for transfers between devices: 119 us -> none
    all_to_all x1 -> x4, blocking collectives: 224 us -> 119 us  [the longest x1 46.2 us: per_device(): seats = exchange(seats, 'node')]
    ppermute x0 -> x1, starting transfers between devices: none -> 16.1 us  [per_device(): other = lax.ppermute(own, 'core', [(0, 1), (1, 0)])]
    scatter-add x1 -> x0, other arithmetic: 8.7 us -> none  [combine(): jax.ops.segment_sum(scaled.reshape(-1, features), owners.reshape(-1), num...]
    all_to_all x1 -> x0, starting transfers between devices: 7.7 us -> none  [per_device(): lax.all_to_all(partial_value.reshape(row_block.shape), 'node', split_axis...]
  transfers between devices with their start and end apart: 2 -> 1, of which waited for: 2 -> 0; matrix products, arithmetic and copies ran while one was open for 0% -> 0% of each run, Pallas kernels for 0% -> 1%
where the time goes in v1:
time: 143 us; the launch traced here: 142 us
  blocking collectives  119 us (83%)
  starting transfers between devices  16.1 us (11%)
  Pallas kernels  5.53 us (4%)
  other arithmetic  1.9 us (1%)
    all_to_all x1, blocking collectives, per_device(): seats = exchange(seats, 'node')  46.2 us
    all_to_all x1, blocking collectives, per_device(): exchange(total.reshape(2 * NODES, HALF // 2, LANES), ('node', 'core'))  34.5 us
    all_to_all x1, blocking collectives, per_device(): rows = exchange(jnp.broadcast_to(mine, (CHIPS, ROWS, LANES)), ('x', 'cuts'))  21.5 us
    all_to_all x1, blocking collectives, per_device(): parts = exchange(parts, ('x', 'cuts'))  16.3 us
    ppermute x1, starting transfers between devices, per_device(): other = lax.ppermute(own, 'core', [(0, 1), (1, 0)])  16.1 us
    pallas_call x4, Pallas kernels, call(): pl.pallas_call(kernel, out_shape=shapes if many else shapes[0], in_specs=...  5.53 us
  transfers between devices with their start and end apart: 1, of which 0 were waited for; matrix products, arithmetic and copies ran while one was open for 0% of the time, Pallas kernels for 1%

profile of v1, /device:TPU:1, one launch (start us, length us, event | category | flops | bytes accessed | tf_op | source)
XLA Modules:
  0.0 142.3 jit_solution(18308042460661497034)
XLA Ops:
  0.0 0.0 copy-start
  0.0 0.0 copy-start.1
  0.0 0.0 copy-start.2
  0.0 1.8 %pad_maximum_fusion.own_ref = bf16[576,2048]{1,0:T(8,128)(2,1)S(1)} fusion(bf16[192,2048]{1,0:T(8,128)(2,1)} %bitcast.20, bf16[192,2048]{1,0:T(8,128)(2,1)} %bitcast.21, bf16[192,2048]{1,0:T(8,128)(2,1)} %bitcast.22), kind=kLoop, calls=%fused_computation | loop fusion | flops 7077888 | bytes 4718592 | tf_op jit(solution)/shard_map/concatenate | solution.py:128
  1.8 16.1 %collective-permute-start = (bf16[576,2048]{1,0:T(8,128)(2,1)S(1)}, bf16[576,2048]{1,0:T(8,128)(2,1)}, u32[]{:S(2)}, u32[]{:S(2)}) collective-permute-start(bf16[576,2048]{1,0:T(8,128)(2,1)S(1)} %pad_maximum_fusion.own_ref), channel_id=1, source_target_pairs={{0,4},{4,0},{1,5},{5,1},{2,6},{6,2},{3,7},{7,3},{8,12},{12,8},{9,1... | collective-permute-start | bytes 7077896 | tf_op jit(solution)/shard_map/ppermute | solution.py:129
  17.9 0.1 pad_add_fusion.where_ref
  18.0 0.0 copy-done
  18.0 0.0 copy-done.1
  18.0 0.0 copy-done.2
  18.0 0.8 shard_map.64
  18.9 46.2 %all_to_all.20.scale_ref = bf16[32,16,128]{2,1,0:T(8,128)(2,1)S(1)} all-to-all(bf16[32,16,128]{2,1,0:T(8,128)(2,1)S(1)} %get-tuple-element.7), channel_id=1, replica_groups=mesh['node'=32,'x'=4,'core'=2,'cuts'=4] {'node'}, dimensions={0} | all-to-all | bytes 262144 | tf_op jit(solution)/shard_map/all_to_all | solution.py:143
  65.1 0.2 broadcast_in_dim.8
  65.3 21.5 %all_to_all.21.x_ref = bf16[16,256,128]{2,1,0:T(8,128)(2,1)S(1)} all-to-all(bf16[16,256,128]{2,1,0:T(8,128)(2,1)S(1)} %broadcast_in_dim.8), channel_id=1, replica_groups=mesh['node'=32,'x'=4,'core'=2,'cuts'=4] {'x','cuts'}, dimensions={0} | all-to-all | bytes 2097152 | tf_op jit(solution)/shard_map/all_to_all | solution.py:145
  86.9 0.0 collective-permute-done.other_ref
  86.9 3.7 %shard_map.65 = bf16[16,256,128]{2,1,0:T(8,128)(2,1)S(1)} custom-call(bf16[16,256,128]{2,1,0:T(8,128)(2,1)S(1)} %all_to_all.21.x_ref, bf16[32,16,128]{2,1,0:T(8,128)(2,1)S(1)} %all_to_all.20.scale_ref, bf16[576,2048]{1,0:T(8,128)(2,1)S(1)} %pad_maximum_fusion.own_ref, bf16[576,2048]{1,0:T(8,128)(2,1)} %collective-permute-done.other_ref), custom_call_target="tpu_custom_call" | custom-call | tf_op jit(solution)/shard_map/pallas_call | solution.py:116
  90.5 16.3 %all_to_all.22.in_ref = bf16[16,256,128]{2,1,0:T(8,128)(2,1)S(1)} all-to-all(bf16[16,256,128]{2,1,0:T(8,128)(2,1)S(1)} %shard_map.65), channel_id=1, replica_groups=mesh['node'=32,'x'=4,'core'=2,'cuts'=4] {'x','cuts'}, dimensions={0} | all-to-all | bytes 2097152 | tf_op jit(solution)/shard_map/all_to_all | solution.py:147
  106.8 0.2 shard_map.66
  107.0 34.5 %all_to_all.23 = bf16[64,4,128]{2,1,0:T(4,128)(2,1)S(1)} all-to-all(bf16[64,4,128]{2,1,0:T(4,128)(2,1)S(1)} %bitcast.16), channel_id=1, replica_groups=mesh['node'=32,'x'=4,'core'=2,'cuts'=4] {'node','core'}, dimensions={0} | all-to-all | bytes 131072 | tf_op jit(solution)/shard_map/all_to_all | solution.py:149
  141.5 0.8 shard_map.67
  (2 shorter events, 0.0 us)
Async XLA Ops:
  0.0 18.0 %copy-start = (bf16[128,2048]{1,0:T(8,128)(2,1)S(1)}, bf16[128,2048]{1,0:T(8,128)(2,1)}, u32[]{:S(2)}) copy-start(bf16[128,2048]{1,0:T(8,128)(2,1)} %param.6) | copy-start | bytes 1572868
  0.0 18.0 %copy-start.1 = (s32[128,8]{0,1:T(8,128)S(1)}, s32[128,8]{0,1:T(8,128)}, u32[]{:S(2)}) copy-start(s32[128,8]{0,1:T(8,128)} %param.7) | copy-start | bytes 12292
  0.0 18.0 %copy-start.2 = (f32[128,8]{0,1:T(8,128)S(1)}, f32[128,8]{0,1:T(8,128)}, u32[]{:S(2)}) copy-start(f32[128,8]{0,1:T(8,128)} %param.8) | copy-start | bytes 12292
  1.8 85.0 %collective-permute-start = (bf16[576,2048]{1,0:T(8,128)(2,1)S(1)}, bf16[576,2048]{1,0:T(8,128)(2,1)}, u32[]{:S(2)}, u32[]{:S(2)}) collective-permute-start(bf16[576,2048]{1,0:T(8,128)(2,1)S(1)} %pad_maximum_fusion.own_ref), channel_id=1, source_target_pairs={{0,4},{4,0},{1,5},{5,1},{2,6},{6,2},{3,7},{7,3},{8,12},{12,8},{9,1... | collective-permute-start | bytes 7077896 | tf_op jit(solution)/shard_map/ppermute | solution.py:129

commit v2 on v1

v2 whole, which is shorter than its diff:
```python
import functools

import jax
import jax.numpy as jnp
from jax import lax
from jax.experimental import pallas as pl
from jax.experimental.pallas import tpu as pltpu
from jax.sharding import Mesh, PartitionSpec as P

F32 = jnp.float32
BF16 = jnp.bfloat16
NODES = 32
CHIPS = 16
HALF = 8
LANES = 128
WIDTH = 2048
FF = 192
ROWS = NODES * HALF

VMEM = pl.BlockSpec(memory_space=pltpu.VMEM)
SMEM = pl.BlockSpec(memory_space=pltpu.SMEM)
PARAMS = pltpu.CompilerParams(vmem_limit_bytes=16 * 1024 * 1024)


def seat_kernel(where_ref, ids_ref, route_ref, tok_ref, out_ref, scale_ref, pos_ref):
    core = where_ref[0]
    column = where_ref[1]
    tokens = tok_ref.shape[0]
    groups = lax.broadcasted_iota(jnp.int32, (NODES, tokens), 0)
    named = jnp.zeros((NODES, tokens), F32)
    weight = jnp.zeros((NODES, tokens), F32)
    for k in range(ids_ref.shape[0]):
        ids = ids_ref[k : k + 1, :]
        hit = (ids >> 2) == groups
        named = jnp.where(hit, 1.0, named)
        weight = weight + jnp.where(hit & ((ids & 3) == column), route_ref[k : k + 1, :], 0.0)
    before = lax.broadcasted_iota(jnp.int32, (tokens, tokens), 0) < lax.broadcasted_iota(
        jnp.int32, (tokens, tokens), 1
    )
    rank = jnp.dot(named.astype(BF16), before.astype(F32).astype(BF16), preferred_element_type=F32)
    pos = jnp.where(named > 0.0, rank, -1.0)
    pos_ref[...] = pos
    seat = lax.broadcasted_iota(jnp.int32, (1, HALF, 1), 1)
    seated = pos[:, None, :] == (seat + core * HALF).astype(F32)
    rows = jnp.where(seated, 1.0, 0.0).reshape(ROWS, tokens).astype(BF16)
    picked = jnp.dot(rows, tok_ref[...], preferred_element_type=F32)
    out_ref[...] = picked.reshape(NODES, HALF, LANES).astype(BF16)
    scale = jnp.sum(jnp.where(seated, weight[:, None, :], 0.0), axis=2, keepdims=True)
    lane = lax.broadcasted_iota(jnp.int32, (1, 1, LANES), 2)
    scale = jnp.sum(jnp.where(lane == seat, scale, 0.0), axis=1)
    high = scale.astype(BF16)
    scale_ref[0] = high
    scale_ref[1] = (scale - high.astype(F32)).astype(BF16)


def copies_kernel(in_ref, out_ref):
    rows = in_ref[...].reshape(ROWS, LANES)
    for q in range(CHIPS):
        out_ref[q] = rows


def expert_kernel(x_ref, scale_ref, gate0, up0, down0, gate1, up1, down1, out_ref):
    x = jnp.concatenate([x_ref[q] for q in range(CHIPS)], axis=1)
    scale = scale_ref[...]
    lane = lax.broadcasted_iota(jnp.int32, (1, HALF, LANES), 2)
    seat = lax.broadcasted_iota(jnp.int32, (1, HALF, LANES), 1)
    scale = jnp.sum(jnp.where(lane == seat, scale[:, None, :], 0.0), axis=2, keepdims=True)
    scale = scale.reshape(ROWS, 1)
    turned = (((1,), (1,)), ((), ()))
    hidden = []
    for gate_ref, up_ref in ((gate0, up0), (gate1, up1)):
        gate = lax.dot_general(x, gate_ref[...], turned, preferred_element_type=F32)
        up = lax.dot_general(x, up_ref[...], turned, preferred_element_type=F32)
        hidden.append((gate / (1.0 + jnp.exp(-gate)) * up).astype(BF16))
    half = ROWS // 2
    low = lax.broadcasted_iota(jnp.int32, (half, LANES), 1) < 64
    for i in range(8):
        cols = slice(i * 256, (i + 1) * 256)
        part = jnp.dot(hidden[0], down0[:, cols], preferred_element_type=F32) + jnp.dot(hidden[1], down1[:, cols], preferred_element_type=F32)
        part = part * scale
        for b in range(2):
            one = part[:half, b * LANES : (b + 1) * LANES]
            two = part[half:, b * LANES : (b + 1) * LANES]
            mixed = pltpu.roll(jnp.where(low, two, one), 64, 1)
            out_ref[4 * i + 2 * b] = jnp.where(low, one, mixed).astype(BF16)
            out_ref[4 * i + 2 * b + 1] = jnp.where(low, mixed, two).astype(BF16)


def sum_kernel(in_ref, out_ref):
    sums = []
    for core in range(2):
        total = 0.0
        for q in range(CHIPS):
            total = total + in_ref[(q // 4 * 2 + core) * 4 + q % 4].astype(F32)
        sums.append(total)
    one, two = sums
    low = lax.broadcasted_iota(jnp.int32, one.shape, 1) < 64
    mixed = pltpu.roll(jnp.where(low, two, one), 64, 1)
    out_ref[0] = jnp.where(low, one, mixed).astype(BF16)
    out_ref[1] = jnp.where(low, mixed, two).astype(BF16)


def mix_kernel(in_ref, pos_ref, out_ref):
    tokens = pos_ref.shape[1]
    pos = pos_ref[...]
    seat = lax.broadcasted_iota(jnp.int32, (1, HALF, 1), 1)
    values = in_ref[...]
    parts = []
    for core in range(2):
        seated = pos[:, None, :] == (seat + core * HALF).astype(F32)
        seated = jnp.where(seated, 1.0, 0.0).reshape(ROWS, tokens).astype(BF16)
        parts.append(
            lax.dot_general(
                values, seated, (((0,), (0,)), ((), ())), preferred_element_type=F32
            )
        )
    out_ref[...] = (parts[0][0:64] + parts[1][64:128]).astype(BF16)


def call(kernel, outs, *args, specs=None, cost=None):
    shapes = [jax.ShapeDtypeStruct(s, d) for s, d in outs]
    many = len(shapes) > 1
    return pl.pallas_call(
        kernel,
        out_shape=shapes if many else shapes[0],
        in_specs=specs or [VMEM] * len(args),
        out_specs=[VMEM] * len(shapes) if many else VMEM,
        compiler_params=PARAMS,
        cost_estimate=cost,
    )(*args)


def per_device(tokens, expert_ids, route_weight, gate_weight, up_weight, down_weight):
    x, core, column = lax.axis_index("x"), lax.axis_index("core"), lax.axis_index("cuts")
    exchange = functools.partial(lax.all_to_all, split_axis=0, concat_axis=0, tiled=True)
    weights = (gate_weight[0].T, up_weight[0].T, down_weight[0])
    pairs = [(0, 1), (1, 0)]
    weights = weights + tuple(lax.ppermute(w, "core", pairs) for w in weights)
    chip = x * 4 + column
    block = lax.dynamic_slice_in_dim(tokens, chip * LANES, LANES, axis=1)
    where = jnp.stack([core, column]).astype(jnp.int32)
    seats, scale, pos = call(
        seat_kernel,
        [
            ((NODES, HALF, LANES), BF16),
            ((2, NODES, LANES), BF16),
            ((NODES, tokens.shape[0]), F32),
        ],
        where,
        expert_ids.T,
        route_weight.T,
        block,
        specs=[SMEM, VMEM, VMEM, VMEM],
    )
    scale = jnp.swapaxes(scale, 0, 1).reshape(NODES, 1, 2, LANES)
    seats = jnp.concatenate([seats.reshape(NODES, 4, 2, LANES), scale], axis=1)
    seats = exchange(seats, "node")
    scale = seats[:, 4, 0].astype(F32) + seats[:, 4, 1].astype(F32)
    copies = call(
        copies_kernel,
        [((CHIPS, ROWS, LANES), BF16)],
        seats[:, :4].reshape(NODES, HALF, LANES),
        cost=pl.CostEstimate(flops=1 << 20, bytes_accessed=1 << 20, transcendentals=0),
    )
    copies, scale, weights = lax.optimization_barrier((copies, scale, weights))
    rows = exchange(copies, ("x", "cuts"))
    plane = ("x", "core", "cuts")
    parts = call(expert_kernel, [((2 * CHIPS, ROWS // 2, LANES), BF16)], rows, scale, *weights)
    parts = exchange(parts, plane)
    total = call(sum_kernel, [((2, ROWS // 2, LANES), BF16)], parts)
    answers = exchange(total.reshape(NODES, HALF, LANES), "node")
    mixed = call(mix_kernel, [((64, tokens.shape[0]), BF16)], answers.reshape(ROWS, LANES), pos)
    return mixed.T


def solution(mesh):
    fine = Mesh(mesh.devices.reshape(NODES, 4, 2, 4), ("node", "x", "core", "cuts"))
    in_specs = (
        P("node", None),
        P("node", None),
        P("node", None),
        P(("node", "cuts"), None, ("x", "core")),
        P(("node", "cuts"), None, ("x", "core")),
        P(("node", "cuts"), ("x", "core"), None),
    )
    out_specs = P("node", ("x", "core", "cuts"))
    return jax.shard_map(
        per_device, mesh=fine, in_specs=in_specs, out_specs=out_specs, check_vma=False
    )
```

time: 143 us -> 136 us (0.951)
  blocking collectives: 119 us -> 73.2 us
  starting transfers between devices: 16.1 us -> 36.5 us
  waiting for transfers between devices: 0.01 us -> 17.7 us
  local copies, waits for them, and re-layouts: 0.22 us -> 1.77 us
  Pallas kernels: 5.53 us -> 4.09 us
    all_to_all x4 -> x3, blocking collectives: 119 us -> 73.2 us  [the longest x1 28.3 us: per_device(): answers = exchange(total.reshape(NODES, HALF, LANES), 'node')]
    all_to_all x0 -> x1, starting transfers between devices: none -> 29.3 us  [per_device(): seats = exchange(seats, 'node')]
    all_to_all x0 -> x1, waiting for transfers between devices: none -> 17.7 us  [per_device(): seats = exchange(seats, 'node')]
    ppermute x1 -> x3, starting transfers between devices: 16.1 us -> 7.2 us  [per_device(): weights = weights + tuple((lax.ppermute(w, 'core', pairs) for w in weights))]
    unnamed x6 -> x12, local copies, waits for them, and re-layouts: 0.01 us -> 1.67 us
    pallas_call x4 -> x5, Pallas kernels: 5.53 us -> 4.09 us  [call(): pl.pallas_call(kernel, out_shape=shapes if many else shapes[0], in_specs=...]
  transfers between devices with their start and end apart: 1 -> 4, of which waited for: 0 -> 1; matrix products, arithmetic and copies ran while one was open for 0% -> 0% of each run, Pallas kernels for 1% -> 0%
where the time goes in v2:
time: 136 us; the launch traced here: 134 us
  blocking collectives  73.2 us (54%)
  starting transfers between devices  36.5 us (27%)
  waiting for transfers between devices  17.7 us (13%)
  Pallas kernels  4.09 us (3%)
  local copies, waits for them, and re-layouts  1.77 us (1%)
    all_to_all x1, starting transfers between devices, per_device(): seats = exchange(seats, 'node')  29.3 us
    all_to_all x1, blocking collectives, per_device(): answers = exchange(total.reshape(NODES, HALF, LANES), 'node')  28.3 us
    all_to_all x1, blocking collectives, per_device(): parts = exchange(parts, plane)  24.5 us
    all_to_all x1, blocking collectives, per_device(): rows = exchange(copies, ('x', 'cuts'))  20.4 us
    all_to_all x1, waiting for transfers between devices, per_device(): seats = exchange(seats, 'node')  17.7 us
    ppermute x3, starting transfers between devices, per_device(): weights = weights + tuple((lax.ppermute(w, 'core', pairs) for w in weights))  7.2 us
    pallas_call x5, Pallas kernels, call(): pl.pallas_call(kernel, out_shape=shapes if many else shapes[0], in_specs=...  4.09 us
  transfers between devices with their start and end apart: 4, of which 1 were waited for; matrix products, arithmetic and copies ran while one was open for 0% of the time, Pallas kernels for 0%

profile of v2, /device:TPU:1, one launch (start us, length us, event | category | flops | bytes accessed | tf_op | source)
XLA Modules:
  0.0 134.2 jit_solution(17511017113204339575)
XLA Ops:
  0.0 0.1 pad_add_fusion.where_ref
  0.1 1.0 copy-done
  1.1 0.7 copy-done.4
  1.7 0.0 copy-done.5
  1.7 0.8 shard_map.64
  2.6 0.7 pad_maximum_fusion
  3.4 29.3 %all-to-all-start = ((bf16[32,5,2,128]{3,2,1,0:T(2,128)(2,1)}), bf16[32,5,2,128]{3,2,1,0:T(2,128)(2,1)S(1)}, u32[]{:S(2)}, u32[]{:S(2)}) async-start(bf16[32,5,2,128]{3,2,1,0:T(2,128)(2,1)} %pad_maximum_fusion), calls=%async_computation | async-start | bytes 163840 | tf_op jit(solution)/shard_map/all_to_all | solution.py:157
  32.7 2.9 %collective-permute-start = (bf16[192,2048]{1,0:T(8,128)(2,1)}, bf16[192,2048]{1,0:T(8,128)(2,1)S(1)}, u32[]{:S(2)}, u32[]{:S(2)}) collective-permute-start(bf16[192,2048]{1,0:T(8,128)(2,1)} %bitcast.21), channel_id=1, source_target_pairs={{0,4},{4,0},{1,5},{5,1},{2,6},{6,2},{3,7},{7,3},{8,12},{12,8},{9,1... | collective-permute-start | bytes 2359304 | tf_op jit(solution)/shard_map/ppermute | solution.py:138
  35.5 1.9 %collective-permute-start.1 = (bf16[192,2048]{1,0:T(8,128)(2,1)}, bf16[192,2048]{1,0:T(8,128)(2,1)S(1)}, u32[]{:S(2)}, u32[]{:S(2)}) collective-permute-start(bf16[192,2048]{1,0:T(8,128)(2,1)} %bitcast.23), channel_id=1, source_target_pairs={{0,4},{4,0},{1,5},{5,1},{2,6},{6,2},{3,7},{7,3},{8,12},{12,8},{9,1... | collective-permute-start | bytes 2359304 | tf_op jit(solution)/shard_map/ppermute | solution.py:138
  37.5 2.4 %collective-permute-start.2 = (bf16[192,2048]{1,0:T(8,128)(2,1)}, bf16[192,2048]{1,0:T(8,128)(2,1)S(1)}, u32[]{:S(2)}, u32[]{:S(2)}) collective-permute-start(bf16[192,2048]{1,0:T(8,128)(2,1)} %bitcast.25), channel_id=1, source_target_pairs={{0,4},{4,0},{1,5},{5,1},{2,6},{6,2},{3,7},{7,3},{8,12},{12,8},{9,1... | collective-permute-start | bytes 2359304 | tf_op jit(solution)/shard_map/ppermute | solution.py:138
  39.9 17.7 %all-to-all-done = bf16[32,5,2,128]{3,2,1,0:T(2,128)(2,1)S(1)} async-done(((bf16[32,5,2,128]{3,2,1,0:T(2,128)(2,1)}), bf16[32,5,2,128]{3,2,1,0:T(2,128)(2,1)S(1)}, u32[]{:S(2)}, u32[]{:S(2)}) %all-to-all-start) | async-done | bytes 81952 | tf_op jit(solution)/shard_map/all_to_all | solution.py:157
  57.6 0.0 copy-start.3
  57.6 0.2 shard_map.65
  57.9 0.0 copy-start.1
  57.9 0.0 copy-start.2
  57.9 0.0 collective-permute-done.gate1
  57.9 0.0 collective-permute-done.1.up1
  57.9 0.0 collective-permute-done.2.down1
  57.9 20.4 %all_to_all.20.x_ref = bf16[16,256,128]{2,1,0:T(8,128)(2,1)S(1)} all-to-all(bf16[16,256,128]{2,1,0:T(8,128)(2,1)S(1)} %shard_map.65), channel_id=1, replica_groups=mesh['node'=32,'x'=4,'core'=2,'cuts'=4] {'x','cuts'}, dimensions={0} | all-to-all | bytes 2097152 | tf_op jit(solution)/shard_map/all_to_all | solution.py:166
  78.3 2.0 %shard_map.66 = bf16[32,128,128]{2,1,0:T(8,128)(2,1)S(1)} custom-call(bf16[16,256,128]{2,1,0:T(8,128)(2,1)S(1)} %all_to_all.20.x_ref, f32[32,128]{1,0:T(8,128)S(1)} %add_bitcast_fusion.scale_ref, bf16[192,2048]{1,0:T(8,128)(2,1)S(1)} %bitcast.22, bf16[192,2048]{1,0:T(8,128)(2,1)S(1)} %bitcast.24, bf16[192,2048]{1,0:T(8,128)(2,1)S(1)} %bitcast.26, ...), custom_call_target="tpu_custom_call" | custom-call | tf_op jit(solution)/shard_map/pallas_call | solution.py:123
  80.3 24.5 %all_to_all.21.in_ref = bf16[32,128,128]{2,1,0:T(8,128)(2,1)S(1)} all-to-all(bf16[32,128,128]{2,1,0:T(8,128)(2,1)S(1)} %shard_map.66), channel_id=1, replica_groups=mesh['node'=32,'x'=4,'core'=2,'cuts'=4] {'x','core','cuts'}, dimensions={0} | all-to-all | bytes 2097152 | tf_op jit(solution)/shard_map/all_to_all | solution.py:169
  104.8 0.2 shard_map.67
  105.1 28.3 %all_to_all.22 = bf16[32,8,128]{2,1,0:T(8,128)(2,1)S(1)} all-to-all(bf16[32,8,128]{2,1,0:T(8,128)(2,1)S(1)} %bitcast.27), channel_id=1, replica_groups=mesh['node'=32,'x'=4,'core'=2,'cuts'=4] {'node'}, dimensions={0} | all-to-all | bytes 131072 | tf_op jit(solution)/shard_map/all_to_all | solution.py:171
  133.4 0.8 shard_map.68
  (11 shorter events, 0.1 us)
Async XLA Ops:
  0.0 1.0 copy-start
  1.0 0.7 copy-start.4
  1.0 0.7 copy-start.5
  3.4 54.2 %all-to-all-start = ((bf16[32,5,2,128]{3,2,1,0:T(2,128)(2,1)}), bf16[32,5,2,128]{3,2,1,0:T(2,128)(2,1)S(1)}, u32[]{:S(2)}, u32[]{:S(2)}) async-start(bf16[32,5,2,128]{3,2,1,0:T(2,128)(2,1)} %pad_maximum_fusion), calls=%async_computation | async-start | bytes 163840 | tf_op jit(solution)/shard_map/all_to_all | solution.py:157
  32.7 25.2 %collective-permute-start = (bf16[192,2048]{1,0:T(8,128)(2,1)}, bf16[192,2048]{1,0:T(8,128)(2,1)S(1)}, u32[]{:S(2)}, u32[]{:S(2)}) collective-permute-start(bf16[192,2048]{1,0:T(8,128)(2,1)} %bitcast.21), channel_id=1, source_target_pairs={{0,4},{4,0},{1,5},{5,1},{2,6},{6,2},{3,7},{7,3},{8,12},{12,8},{9,1... | collective-permute-start | bytes 2359304 | tf_op jit(solution)/shard_map/ppermute | solution.py:138
  35.5 22.4 %collective-permute-start.1 = (bf16[192,2048]{1,0:T(8,128)(2,1)}, bf16[192,2048]{1,0:T(8,128)(2,1)S(1)}, u32[]{:S(2)}, u32[]{:S(2)}) collective-permute-start(bf16[192,2048]{1,0:T(8,128)(2,1)} %bitcast.23), channel_id=1, source_target_pairs={{0,4},{4,0},{1,5},{5,1},{2,6},{6,2},{3,7},{7,3},{8,12},{12,8},{9,1... | collective-permute-start | bytes 2359304 | tf_op jit(solution)/shard_map/ppermute | solution.py:138
  37.5 20.5 %collective-permute-start.2 = (bf16[192,2048]{1,0:T(8,128)(2,1)}, bf16[192,2048]{1,0:T(8,128)(2,1)S(1)}, u32[]{:S(2)}, u32[]{:S(2)}) collective-permute-start(bf16[192,2048]{1,0:T(8,128)(2,1)} %bitcast.25), channel_id=1, source_target_pairs={{0,4},{4,0},{1,5},{5,1},{2,6},{6,2},{3,7},{7,3},{8,12},{12,8},{9,1... | collective-permute-start | bytes 2359304 | tf_op jit(solution)/shard_map/ppermute | solution.py:138
  57.6 20.7 %copy-start.3 = (bf16[1,192,2048]{2,1,0:T(8,128)(2,1)S(1)}, bf16[1,192,2048]{2,1,0:T(8,128)(2,1)}, u32[]{:S(2)}) copy-start(bf16[1,192,2048]{2,1,0:T(8,128)(2,1)} %param.11) | copy-start | bytes 2359300
  57.9 20.4 %copy-start.1 = (bf16[1,2048,192]{1,2,0:T(8,128)(2,1)S(1)}, bf16[1,2048,192]{1,2,0:T(8,128)(2,1)}, u32[]{:S(2)}) copy-start(bf16[1,2048,192]{1,2,0:T(8,128)(2,1)} %param.9) | copy-start | bytes 2359300
  57.9 20.4 %copy-start.2 = (bf16[1,2048,192]{1,2,0:T(8,128)(2,1)S(1)}, bf16[1,2048,192]{1,2,0:T(8,128)(2,1)}, u32[]{:S(2)}) copy-start(bf16[1,2048,192]{1,2,0:T(8,128)(2,1)} %param.10) | copy-start | bytes 2359300

commit v3 on v2

--- a/solution.py
+++ b/solution.py
@@ -136,7 +136,7 @@
     weights = (gate_weight[0].T, up_weight[0].T, down_weight[0])
     pairs = [(0, 1), (1, 0)]
     weights = weights + tuple(lax.ppermute(w, "core", pairs) for w in weights)
-    chip = x * 4 + column
+    chip = column * 4 + x
     block = lax.dynamic_slice_in_dim(tokens, chip * LANES, LANES, axis=1)
     where = jnp.stack([core, column]).astype(jnp.int32)
     seats, scale, pos = call(
@@ -163,7 +163,7 @@
         cost=pl.CostEstimate(flops=1 << 20, bytes_accessed=1 << 20, transcendentals=0),
     )
     copies, scale, weights = lax.optimization_barrier((copies, scale, weights))
-    rows = exchange(copies, ("x", "cuts"))
+    rows = exchange(copies, ("cuts", "x"))
     plane = ("x", "core", "cuts")
     parts = call(expert_kernel, [((2 * CHIPS, ROWS // 2, LANES), BF16)], rows, scale, *weights)
     parts = exchange(parts, plane)

time: 136 us -> 135 us (level)
  no operation moved by 1% of the time
where the time goes in v3:
time: 135 us; the launch traced here: 134 us
  blocking collectives  72.9 us (54%)
  starting transfers between devices  36.5 us (27%)
  waiting for transfers between devices  17.7 us (13%)
  Pallas kernels  4.09 us (3%)
  local copies, waits for them, and re-layouts  1.77 us (1%)
    all_to_all x1, starting transfers between devices, per_device(): seats = exchange(seats, 'node')  29.3 us
    all_to_all x1, blocking collectives, per_device(): answers = exchange(total.reshape(NODES, HALF, LANES), 'node')  28.3 us
    all_to_all x1, blocking collectives, per_device(): parts = exchange(parts, plane)  23.5 us
    all_to_all x1, blocking collectives, per_device(): rows = exchange(copies, ('cuts', 'x'))  21.1 us
    all_to_all x1, waiting for transfers between devices, per_device(): seats = exchange(seats, 'node')  17.7 us
    ppermute x3, starting transfers between devices, per_device(): weights = weights + tuple((lax.ppermute(w, 'core', pairs) for w in weights))  7.2 us
    pallas_call x5, Pallas kernels, call(): pl.pallas_call(kernel, out_shape=shapes if many else shapes[0], in_specs=...  4.09 us
  transfers between devices with their start and end apart: 4, of which 1 were waited for; matrix products, arithmetic and copies ran while one was open for 0% of the time, Pallas kernels for 0%

profile of v3, /device:TPU:1, one launch (start us, length us, event | category | flops | bytes accessed | tf_op | source)
XLA Modules:
  0.0 133.9 jit_solution(9006795751252220780)
XLA Ops:
  0.0 0.1 pad_add_fusion.where_ref
  0.1 1.0 copy-done
  1.1 0.7 copy-done.4
  1.7 0.0 copy-done.5
  1.7 0.8 shard_map.64
  2.6 0.7 pad_maximum_fusion
  3.4 29.3 %all-to-all-start = ((bf16[32,5,2,128]{3,2,1,0:T(2,128)(2,1)}), bf16[32,5,2,128]{3,2,1,0:T(2,128)(2,1)S(1)}, u32[]{:S(2)}, u32[]{:S(2)}) async-start(bf16[32,5,2,128]{3,2,1,0:T(2,128)(2,1)} %pad_maximum_fusion), calls=%async_computation | async-start | bytes 163840 | tf_op jit(solution)/shard_map/all_to_all | solution.py:157
  32.7 2.9 %collective-permute-start = (bf16[192,2048]{1,0:T(8,128)(2,1)}, bf16[192,2048]{1,0:T(8,128)(2,1)S(1)}, u32[]{:S(2)}, u32[]{:S(2)}) collective-permute-start(bf16[192,2048]{1,0:T(8,128)(2,1)} %bitcast.21), channel_id=1, source_target_pairs={{0,4},{4,0},{1,5},{5,1},{2,6},{6,2},{3,7},{7,3},{8,12},{12,8},{9,1... | collective-permute-start | bytes 2359304 | tf_op jit(solution)/shard_map/ppermute | solution.py:138
  35.5 1.9 %collective-permute-start.1 = (bf16[192,2048]{1,0:T(8,128)(2,1)}, bf16[192,2048]{1,0:T(8,128)(2,1)S(1)}, u32[]{:S(2)}, u32[]{:S(2)}) collective-permute-start(bf16[192,2048]{1,0:T(8,128)(2,1)} %bitcast.23), channel_id=1, source_target_pairs={{0,4},{4,0},{1,5},{5,1},{2,6},{6,2},{3,7},{7,3},{8,12},{12,8},{9,1... | collective-permute-start | bytes 2359304 | tf_op jit(solution)/shard_map/ppermute | solution.py:138
  37.5 2.4 %collective-permute-start.2 = (bf16[192,2048]{1,0:T(8,128)(2,1)}, bf16[192,2048]{1,0:T(8,128)(2,1)S(1)}, u32[]{:S(2)}, u32[]{:S(2)}) collective-permute-start(bf16[192,2048]{1,0:T(8,128)(2,1)} %bitcast.25), channel_id=1, source_target_pairs={{0,4},{4,0},{1,5},{5,1},{2,6},{6,2},{3,7},{7,3},{8,12},{12,8},{9,1... | collective-permute-start | bytes 2359304 | tf_op jit(solution)/shard_map/ppermute | solution.py:138
  39.9 17.7 %all-to-all-done = bf16[32,5,2,128]{3,2,1,0:T(2,128)(2,1)S(1)} async-done(((bf16[32,5,2,128]{3,2,1,0:T(2,128)(2,1)}), bf16[32,5,2,128]{3,2,1,0:T(2,128)(2,1)S(1)}, u32[]{:S(2)}, u32[]{:S(2)}) %all-to-all-start) | async-done | bytes 81952 | tf_op jit(solution)/shard_map/all_to_all | solution.py:157
  57.6 0.0 copy-start.3
  57.6 0.2 shard_map.65
  57.9 0.0 copy-start.1
  57.9 0.0 copy-start.2
  57.9 0.0 collective-permute-done.gate1
  57.9 0.0 collective-permute-done.1.up1
  57.9 0.0 collective-permute-done.2.down1
  57.9 21.1 %all_to_all.20.x_ref = bf16[16,256,128]{2,1,0:T(8,128)(2,1)S(1)} all-to-all(bf16[16,256,128]{2,1,0:T(8,128)(2,1)S(1)} %shard_map.65), channel_id=1, replica_groups=mesh['node'=32,'x'=4,'core'=2,'cuts'=4] {'cuts','x'}, dimensions={0} | all-to-all | bytes 2097152 | tf_op jit(solution)/shard_map/all_to_all | solution.py:166
  79.1 2.0 %shard_map.66 = bf16[32,128,128]{2,1,0:T(8,128)(2,1)S(1)} custom-call(bf16[16,256,128]{2,1,0:T(8,128)(2,1)S(1)} %all_to_all.20.x_ref, f32[32,128]{1,0:T(8,128)S(1)} %add_bitcast_fusion.scale_ref, bf16[192,2048]{1,0:T(8,128)(2,1)S(1)} %bitcast.22, bf16[192,2048]{1,0:T(8,128)(2,1)S(1)} %bitcast.24, bf16[192,2048]{1,0:T(8,128)(2,1)S(1)} %bitcast.26, ...), custom_call_target="tpu_custom_call" | custom-call | tf_op jit(solution)/shard_map/pallas_call | solution.py:123
  81.1 23.5 %all_to_all.21.in_ref = bf16[32,128,128]{2,1,0:T(8,128)(2,1)S(1)} all-to-all(bf16[32,128,128]{2,1,0:T(8,128)(2,1)S(1)} %shard_map.66), channel_id=1, replica_groups=mesh['node'=32,'x'=4,'core'=2,'cuts'=4] {'x','core','cuts'}, dimensions={0} | all-to-all | bytes 2097152 | tf_op jit(solution)/shard_map/all_to_all | solution.py:169
  104.6 0.2 shard_map.67
  104.8 28.3 %all_to_all.22 = bf16[32,8,128]{2,1,0:T(8,128)(2,1)S(1)} all-to-all(bf16[32,8,128]{2,1,0:T(8,128)(2,1)S(1)} %bitcast.27), channel_id=1, replica_groups=mesh['node'=32,'x'=4,'core'=2,'cuts'=4] {'node'}, dimensions={0} | all-to-all | bytes 131072 | tf_op jit(solution)/shard_map/all_to_all | solution.py:171
  133.1 0.8 shard_map.68
  (11 shorter events, 0.1 us)
Async XLA Ops:
  0.0 1.0 copy-start
  1.0 0.7 copy-start.4
  1.0 0.7 copy-start.5
  3.4 54.2 %all-to-all-start = ((bf16[32,5,2,128]{3,2,1,0:T(2,128)(2,1)}), bf16[32,5,2,128]{3,2,1,0:T(2,128)(2,1)S(1)}, u32[]{:S(2)}, u32[]{:S(2)}) async-start(bf16[32,5,2,128]{3,2,1,0:T(2,128)(2,1)} %pad_maximum_fusion), calls=%async_computation | async-start | bytes 163840 | tf_op jit(solution)/shard_map/all_to_all | solution.py:157
  32.7 25.2 %collective-permute-start = (bf16[192,2048]{1,0:T(8,128)(2,1)}, bf16[192,2048]{1,0:T(8,128)(2,1)S(1)}, u32[]{:S(2)}, u32[]{:S(2)}) collective-permute-start(bf16[192,2048]{1,0:T(8,128)(2,1)} %bitcast.21), channel_id=1, source_target_pairs={{0,4},{4,0},{1,5},{5,1},{2,6},{6,2},{3,7},{7,3},{8,12},{12,8},{9,1... | collective-permute-start | bytes 2359304 | tf_op jit(solution)/shard_map/ppermute | solution.py:138
  35.5 22.4 %collective-permute-start.1 = (bf16[192,2048]{1,0:T(8,128)(2,1)}, bf16[192,2048]{1,0:T(8,128)(2,1)S(1)}, u32[]{:S(2)}, u32[]{:S(2)}) collective-permute-start(bf16[192,2048]{1,0:T(8,128)(2,1)} %bitcast.23), channel_id=1, source_target_pairs={{0,4},{4,0},{1,5},{5,1},{2,6},{6,2},{3,7},{7,3},{8,12},{12,8},{9,1... | collective-permute-start | bytes 2359304 | tf_op jit(solution)/shard_map/ppermute | solution.py:138
  37.5 20.5 %collective-permute-start.2 = (bf16[192,2048]{1,0:T(8,128)(2,1)}, bf16[192,2048]{1,0:T(8,128)(2,1)S(1)}, u32[]{:S(2)}, u32[]{:S(2)}) collective-permute-start(bf16[192,2048]{1,0:T(8,128)(2,1)} %bitcast.25), channel_id=1, source_target_pairs={{0,4},{4,0},{1,5},{5,1},{2,6},{6,2},{3,7},{7,3},{8,12},{12,8},{9,1... | collective-permute-start | bytes 2359304 | tf_op jit(solution)/shard_map/ppermute | solution.py:138
  57.6 21.4 %copy-start.3 = (bf16[1,192,2048]{2,1,0:T(8,128)(2,1)S(1)}, bf16[1,192,2048]{2,1,0:T(8,128)(2,1)}, u32[]{:S(2)}) copy-start(bf16[1,192,2048]{2,1,0:T(8,128)(2,1)} %param.11) | copy-start | bytes 2359300
  57.9 21.2 %copy-start.1 = (bf16[1,2048,192]{1,2,0:T(8,128)(2,1)S(1)}, bf16[1,2048,192]{1,2,0:T(8,128)(2,1)}, u32[]{:S(2)}) copy-start(bf16[1,2048,192]{1,2,0:T(8,128)(2,1)} %param.9) | copy-start | bytes 2359300
  57.9 21.2 %copy-start.2 = (bf16[1,2048,192]{1,2,0:T(8,128)(2,1)S(1)}, bf16[1,2048,192]{1,2,0:T(8,128)(2,1)}, u32[]{:S(2)}) copy-start(bf16[1,2048,192]{1,2,0:T(8,128)(2,1)} %param.10) | copy-start | bytes 2359300

commit v4 on v3

--- a/solution.py
+++ b/solution.py
@@ -10,6 +10,7 @@
 F32 = jnp.float32
 BF16 = jnp.bfloat16
 NODES = 32
+FIRST = 16
 CHIPS = 16
 HALF = 8
 LANES = 128
@@ -26,7 +27,7 @@
     core = where_ref[0]
     column = where_ref[1]
     tokens = tok_ref.shape[0]
-    groups = lax.broadcasted_iota(jnp.int32, (NODES, tokens), 0)
+    groups = (lax.broadcasted_iota(jnp.int32, (NODES, tokens), 0) + FIRST) & (NODES - 1)
     named = jnp.zeros((NODES, tokens), F32)
     weight = jnp.zeros((NODES, tokens), F32)
     for k in range(ids_ref.shape[0]):
@@ -133,6 +134,7 @@
 def per_device(tokens, expert_ids, route_weight, gate_weight, up_weight, down_weight):
     x, core, column = lax.axis_index("x"), lax.axis_index("core"), lax.axis_index("cuts")
     exchange = functools.partial(lax.all_to_all, split_axis=0, concat_axis=0, tiled=True)
+    ring = [[(FIRST + i) % NODES for i in range(NODES)]]
     weights = (gate_weight[0].T, up_weight[0].T, down_weight[0])
     pairs = [(0, 1), (1, 0)]
     weights = weights + tuple(lax.ppermute(w, "core", pairs) for w in weights)
@@ -154,7 +156,7 @@
     )
     scale = jnp.swapaxes(scale, 0, 1).reshape(NODES, 1, 2, LANES)
     seats = jnp.concatenate([seats.reshape(NODES, 4, 2, LANES), scale], axis=1)
-    seats = exchange(seats, "node")
+    seats = exchange(seats, "node", axis_index_groups=ring)
     scale = seats[:, 4, 0].astype(F32) + seats[:, 4, 1].astype(F32)
     copies = call(
         copies_kernel,
@@ -168,7 +170,7 @@
     parts = call(expert_kernel, [((2 * CHIPS, ROWS // 2, LANES), BF16)], rows, scale, *weights)
     parts = exchange(parts, plane)
     total = call(sum_kernel, [((2, ROWS // 2, LANES), BF16)], parts)
-    answers = exchange(total.reshape(NODES, HALF, LANES), "node")
+    answers = exchange(total.reshape(NODES, HALF, LANES), "node", axis_index_groups=ring)
     mixed = call(mix_kernel, [((64, tokens.shape[0]), BF16)], answers.reshape(ROWS, LANES), pos)
     return mixed.T
 

time: 135 us -> 124 us (0.919)
  waiting for transfers between devices: 17.7 us -> 1.73 us
  starting transfers between devices: 36.5 us -> 43.6 us
  blocking collectives: 72.9 us -> 71.3 us
    all_to_all x1, waiting for transfers between devices: 17.7 us -> 0.01 us  [per_device(): seats = exchange(seats, 'node', axis_index_groups=ring)]
    all_to_all x1, starting transfers between devices: 29.3 us -> 36.2 us  [per_device(): seats = exchange(seats, 'node', axis_index_groups=ring)]
    all_to_all x1, blocking collectives: 23.5 us -> 21.1 us  [per_device(): parts = exchange(parts, plane)]
    all_to_all x1, blocking collectives: 21.1 us -> 22.9 us  [per_device(): rows = exchange(copies, ('cuts', 'x'))]
    ppermute x3, waiting for transfers between devices: 0.01 us -> 1.73 us  [per_device(): weights = weights + tuple((lax.ppermute(w, 'core', pairs) for w in weights))]
where the time goes in v4:
time: 124 us
  blocking collectives  71.3 us (58%)
  starting transfers between devices  43.6 us (35%)
  Pallas kernels  4.09 us (3%)
  local copies, waits for them, and re-layouts  1.77 us (1%)
  waiting for transfers between devices  1.73 us (1%)
    all_to_all x1, starting transfers between devices, per_device(): seats = exchange(seats, 'node', axis_index_groups=ring)  36.2 us
    all_to_all x1, blocking collectives, per_device(): exchange(total.reshape(NODES, HALF, LANES), 'node', axis_index_groups=ring)  27.4 us
    all_to_all x1, blocking collectives, per_device(): rows = exchange(copies, ('cuts', 'x'))  22.9 us
    all_to_all x1, blocking collectives, per_device(): parts = exchange(parts, plane)  21.1 us
    ppermute x3, starting transfers between devices, per_device(): weights = weights + tuple((lax.ppermute(w, 'core', pairs) for w in weights))  7.48 us
    pallas_call x5, Pallas kernels, call(): pl.pallas_call(kernel, out_shape=shapes if many else shapes[0], in_specs=...  4.09 us
  transfers between devices with their start and end apart: 4, of which 1 were waited for; matrix products, arithmetic and copies ran while one was open for 0% of the time, Pallas kernels for 0%

profile of v4, /device:TPU:1, one launch (start us, length us, event | category | flops | bytes accessed | tf_op | source)
XLA Modules:
  0.0 123.5 jit_solution(6596111634686381015)
XLA Ops:
  0.0 0.1 pad_add_fusion.where_ref
  0.1 1.0 copy-done
  1.1 0.7 copy-done.4
  1.7 0.0 copy-done.5
  1.7 0.8 shard_map.64
  2.6 0.7 pad_maximum_fusion
  3.4 36.2 %all-to-all-start = ((bf16[32,5,2,128]{3,2,1,0:T(2,128)(2,1)}), bf16[32,5,2,128]{3,2,1,0:T(2,128)(2,1)S(1)}, u32[]{:S(2)}, u32[]{:S(2)}) async-start(bf16[32,5,2,128]{3,2,1,0:T(2,128)(2,1)} %pad_maximum_fusion), calls=%async_computation | async-start | bytes 163840 | tf_op jit(solution)/shard_map/all_to_all | solution.py:159
  39.5 3.1 %collective-permute-start = (bf16[192,2048]{1,0:T(8,128)(2,1)}, bf16[192,2048]{1,0:T(8,128)(2,1)S(1)}, u32[]{:S(2)}, u32[]{:S(2)}) collective-permute-start(bf16[192,2048]{1,0:T(8,128)(2,1)} %bitcast.21), channel_id=1, source_target_pairs={{0,4},{4,0},{1,5},{5,1},{2,6},{6,2},{3,7},{7,3},{8,12},{12,8},{9,1... | collective-permute-start | bytes 2359304 | tf_op jit(solution)/shard_map/ppermute | solution.py:140
  42.7 1.9 %collective-permute-start.1 = (bf16[192,2048]{1,0:T(8,128)(2,1)}, bf16[192,2048]{1,0:T(8,128)(2,1)S(1)}, u32[]{:S(2)}, u32[]{:S(2)}) collective-permute-start(bf16[192,2048]{1,0:T(8,128)(2,1)} %bitcast.23), channel_id=1, source_target_pairs={{0,4},{4,0},{1,5},{5,1},{2,6},{6,2},{3,7},{7,3},{8,12},{12,8},{9,1... | collective-permute-start | bytes 2359304 | tf_op jit(solution)/shard_map/ppermute | solution.py:140
  44.6 2.4 %collective-permute-start.2 = (bf16[192,2048]{1,0:T(8,128)(2,1)}, bf16[192,2048]{1,0:T(8,128)(2,1)S(1)}, u32[]{:S(2)}, u32[]{:S(2)}) collective-permute-start(bf16[192,2048]{1,0:T(8,128)(2,1)} %bitcast.25), channel_id=1, source_target_pairs={{0,4},{4,0},{1,5},{5,1},{2,6},{6,2},{3,7},{7,3},{8,12},{12,8},{9,1... | collective-permute-start | bytes 2359304 | tf_op jit(solution)/shard_map/ppermute | solution.py:140
  47.0 0.0 all-to-all-done
  47.1 0.0 copy-start.3
  47.1 0.2 shard_map.65
  47.4 0.0 copy-start.1
  47.4 0.0 copy-start.2
  47.4 0.0 collective-permute-done.gate1
  47.4 0.0 collective-permute-done.1.up1
  47.4 1.7 %collective-permute-done.2.down1 = bf16[192,2048]{1,0:T(8,128)(2,1)S(1)} collective-permute-done((bf16[192,2048]{1,0:T(8,128)(2,1)}, bf16[192,2048]{1,0:T(8,128)(2,1)S(1)}, u32[]{:S(2)}, u32[]{:S(2)}) %collective-permute-start.2) | collective-permute-done | bytes 786464 | tf_op jit(solution)/shard_map/ppermute | solution.py:140
  49.1 22.9 %all_to_all.20.x_ref = bf16[16,256,128]{2,1,0:T(8,128)(2,1)S(1)} all-to-all(bf16[16,256,128]{2,1,0:T(8,128)(2,1)S(1)} %shard_map.65), channel_id=1, replica_groups=mesh['node'=32,'x'=4,'core'=2,'cuts'=4] {'cuts','x'}, dimensions={0} | all-to-all | bytes 2097152 | tf_op jit(solution)/shard_map/all_to_all | solution.py:168
  72.0 2.0 %shard_map.66 = bf16[32,128,128]{2,1,0:T(8,128)(2,1)S(1)} custom-call(bf16[16,256,128]{2,1,0:T(8,128)(2,1)S(1)} %all_to_all.20.x_ref, f32[32,128]{1,0:T(8,128)S(1)} %add_bitcast_fusion.scale_ref, bf16[192,2048]{1,0:T(8,128)(2,1)S(1)} %bitcast.22, bf16[192,2048]{1,0:T(8,128)(2,1)S(1)} %bitcast.24, bf16[192,2048]{1,0:T(8,128)(2,1)S(1)} %bitcast.26, ...), custom_call_target="tpu_custom_call" | custom-call | tf_op jit(solution)/shard_map/pallas_call | solution.py:124
  74.0 21.1 %all_to_all.21.in_ref = bf16[32,128,128]{2,1,0:T(8,128)(2,1)S(1)} all-to-all(bf16[32,128,128]{2,1,0:T(8,128)(2,1)S(1)} %shard_map.66), channel_id=1, replica_groups=mesh['node'=32,'x'=4,'core'=2,'cuts'=4] {'x','core','cuts'}, dimensions={0} | all-to-all | bytes 2097152 | tf_op jit(solution)/shard_map/all_to_all | solution.py:171
  95.1 0.2 shard_map.67
  95.3 27.4 %all_to_all.22 = bf16[32,8,128]{2,1,0:T(8,128)(2,1)S(1)} all-to-all(bf16[32,8,128]{2,1,0:T(8,128)(2,1)S(1)} %bitcast.27), channel_id=1, replica_groups={{512,544,576,608,640,672,704,736,768,800,832,864,896,928,960,992,0,32,6..., dimensions={0} | all-to-all | bytes 131072 | tf_op jit(solution)/shard_map/all_to_all | solution.py:173
  122.7 0.8 shard_map.68
  (11 shorter events, 0.1 us)
Async XLA Ops:
  0.0 1.0 copy-start
  1.0 0.7 copy-start.4
  1.0 0.7 copy-start.5
  3.4 43.7 %all-to-all-start = ((bf16[32,5,2,128]{3,2,1,0:T(2,128)(2,1)}), bf16[32,5,2,128]{3,2,1,0:T(2,128)(2,1)S(1)}, u32[]{:S(2)}, u32[]{:S(2)}) async-start(bf16[32,5,2,128]{3,2,1,0:T(2,128)(2,1)} %pad_maximum_fusion), calls=%async_computation | async-start | bytes 163840 | tf_op jit(solution)/shard_map/all_to_all | solution.py:159
  39.5 7.9 %collective-permute-start = (bf16[192,2048]{1,0:T(8,128)(2,1)}, bf16[192,2048]{1,0:T(8,128)(2,1)S(1)}, u32[]{:S(2)}, u32[]{:S(2)}) collective-permute-start(bf16[192,2048]{1,0:T(8,128)(2,1)} %bitcast.21), channel_id=1, source_target_pairs={{0,4},{4,0},{1,5},{5,1},{2,6},{6,2},{3,7},{7,3},{8,12},{12,8},{9,1... | collective-permute-start | bytes 2359304 | tf_op jit(solution)/shard_map/ppermute | solution.py:140
  42.7 4.7 %collective-permute-start.1 = (bf16[192,2048]{1,0:T(8,128)(2,1)}, bf16[192,2048]{1,0:T(8,128)(2,1)S(1)}, u32[]{:S(2)}, u32[]{:S(2)}) collective-permute-start(bf16[192,2048]{1,0:T(8,128)(2,1)} %bitcast.23), channel_id=1, source_target_pairs={{0,4},{4,0},{1,5},{5,1},{2,6},{6,2},{3,7},{7,3},{8,12},{12,8},{9,1... | collective-permute-start | bytes 2359304 | tf_op jit(solution)/shard_map/ppermute | solution.py:140
  44.6 4.5 %collective-permute-start.2 = (bf16[192,2048]{1,0:T(8,128)(2,1)}, bf16[192,2048]{1,0:T(8,128)(2,1)S(1)}, u32[]{:S(2)}, u32[]{:S(2)}) collective-permute-start(bf16[192,2048]{1,0:T(8,128)(2,1)} %bitcast.25), channel_id=1, source_target_pairs={{0,4},{4,0},{1,5},{5,1},{2,6},{6,2},{3,7},{7,3},{8,12},{12,8},{9,1... | collective-permute-start | bytes 2359304 | tf_op jit(solution)/shard_map/ppermute | solution.py:140
  47.1 24.9 %copy-start.3 = (bf16[1,192,2048]{2,1,0:T(8,128)(2,1)S(1)}, bf16[1,192,2048]{2,1,0:T(8,128)(2,1)}, u32[]{:S(2)}) copy-start(bf16[1,192,2048]{2,1,0:T(8,128)(2,1)} %param.11) | copy-start | bytes 2359300
  47.4 24.6 %copy-start.1 = (bf16[1,2048,192]{1,2,0:T(8,128)(2,1)S(1)}, bf16[1,2048,192]{1,2,0:T(8,128)(2,1)}, u32[]{:S(2)}) copy-start(bf16[1,2048,192]{1,2,0:T(8,128)(2,1)} %param.9) | copy-start | bytes 2359300
  47.4 24.6 %copy-start.2 = (bf16[1,2048,192]{1,2,0:T(8,128)(2,1)S(1)}, bf16[1,2048,192]{1,2,0:T(8,128)(2,1)}, u32[]{:S(2)}) copy-start(bf16[1,2048,192]{1,2,0:T(8,128)(2,1)} %param.10) | copy-start | bytes 2359300

commit v5 on v4

--- a/solution.py
+++ b/solution.py
@@ -10,7 +10,9 @@
 F32 = jnp.float32
 BF16 = jnp.bfloat16
 NODES = 32
-FIRST = 16
+FIRST = 20
+BACK = 16
+TURN = FIRST - BACK
 CHIPS = 16
 HALF = 8
 LANES = 128
@@ -40,7 +42,7 @@
     )
     rank = jnp.dot(named.astype(BF16), before.astype(F32).astype(BF16), preferred_element_type=F32)
     pos = jnp.where(named > 0.0, rank, -1.0)
-    pos_ref[...] = pos
+    pos_ref[...] = pltpu.roll(pos, TURN, 0)
     seat = lax.broadcasted_iota(jnp.int32, (1, HALF, 1), 1)
     seated = pos[:, None, :] == (seat + core * HALF).astype(F32)
     rows = jnp.where(seated, 1.0, 0.0).reshape(ROWS, tokens).astype(BF16)
@@ -97,8 +99,11 @@
     one, two = sums
     low = lax.broadcasted_iota(jnp.int32, one.shape, 1) < 64
     mixed = pltpu.roll(jnp.where(low, two, one), 64, 1)
-    out_ref[0] = jnp.where(low, one, mixed).astype(BF16)
-    out_ref[1] = jnp.where(low, mixed, two).astype(BF16)
+    rows = (jnp.where(low, one, mixed).astype(BF16), jnp.where(low, mixed, two).astype(BF16))
+    turn, stay = TURN * HALF, rows[0].shape[0] - TURN * HALF
+    for half in range(2):
+        out_ref[half, turn:] = rows[half][:stay]
+        out_ref[1 - half, :turn] = rows[half][stay:]
 
 
 def mix_kernel(in_ref, pos_ref, out_ref):
@@ -134,7 +139,8 @@
 def per_device(tokens, expert_ids, route_weight, gate_weight, up_weight, down_weight):
     x, core, column = lax.axis_index("x"), lax.axis_index("core"), lax.axis_index("cuts")
     exchange = functools.partial(lax.all_to_all, split_axis=0, concat_axis=0, tiled=True)
-    ring = [[(FIRST + i) % NODES for i in range(NODES)]]
+    out_ring = [[(FIRST + i) % NODES for i in range(NODES)]]
+    back_ring = [[(BACK + i) % NODES for i in range(NODES)]]
     weights = (gate_weight[0].T, up_weight[0].T, down_weight[0])
     pairs = [(0, 1), (1, 0)]
     weights = weights + tuple(lax.ppermute(w, "core", pairs) for w in weights)
@@ -156,7 +162,7 @@
     )
     scale = jnp.swapaxes(scale, 0, 1).reshape(NODES, 1, 2, LANES)
     seats = jnp.concatenate([seats.reshape(NODES, 4, 2, LANES), scale], axis=1)
-    seats = exchange(seats, "node", axis_index_groups=ring)
+    seats = exchange(seats, "node", axis_index_groups=out_ring)
     scale = seats[:, 4, 0].astype(F32) + seats[:, 4, 1].astype(F32)
     copies = call(
         copies_kernel,
@@ -170,7 +176,9 @@
     parts = call(expert_kernel, [((2 * CHIPS, ROWS // 2, LANES), BF16)], rows, scale, *weights)
     parts = exchange(parts, plane)
     total = call(sum_kernel, [((2, ROWS // 2, LANES), BF16)], parts)
-    answers = exchange(total.reshape(NODES, HALF, LANES), "node", axis_index_groups=ring)
+    answers = exchange(
+        total.reshape(NODES, HALF, LANES), "node", axis_index_groups=back_ring
+    )
     mixed = call(mix_kernel, [((64, tokens.shape[0]), BF16)], answers.reshape(ROWS, LANES), pos)
     return mixed.T
 

time: 124 us -> 123 us (level)
  starting transfers between devices: 43.6 us -> 38.8 us
  waiting for transfers between devices: 1.73 us -> 4.7 us
    all_to_all x1, starting transfers between devices: 36.2 us -> 31.3 us  [per_device(): seats = exchange(seats, 'node', axis_index_groups=out_ring)]
    all_to_all x1, waiting for transfers between devices: 0.01 us -> 4.69 us  [per_device(): seats = exchange(seats, 'node', axis_index_groups=out_ring)]
    ppermute x3, waiting for transfers between devices: 1.73 us -> 0.01 us  [per_device(): weights = weights + tuple((lax.ppermute(w, 'core', pairs) for w in weights))]
where the time goes in v5:
time: 123 us; the launch traced here: 122 us
  blocking collectives  71.9 us (58%)
  starting transfers between devices  38.8 us (32%)
  waiting for transfers between devices  4.7 us (4%)
  Pallas kernels  4.09 us (3%)
  local copies, waits for them, and re-layouts  1.77 us (1%)
    all_to_all x1, starting transfers between devices, per_device(): seats = exchange(seats, 'node', axis_index_groups=out_ring)  31.3 us
    all_to_all x1, blocking collectives, per_device(): exchange(total.reshape(NODES, HALF, LANES), 'node', axis_index_groups=bac...  27.8 us
    all_to_all x1, blocking collectives, per_device(): rows = exchange(copies, ('cuts', 'x'))  22.2 us
    all_to_all x1, blocking collectives, per_device(): parts = exchange(parts, plane)  22 us
    ppermute x3, starting transfers between devices, per_device(): weights = weights + tuple((lax.ppermute(w, 'core', pairs) for w in weights))  7.48 us
    all_to_all x1, waiting for transfers between devices, per_device(): seats = exchange(seats, 'node', axis_index_groups=out_ring)  4.69 us
    pallas_call x5, Pallas kernels, call(): pl.pallas_call(kernel, out_shape=shapes if many else shapes[0], in_specs=...  4.09 us
  transfers between devices with their start and end apart: 4, of which 1 were waited for; matrix products, arithmetic and copies ran while one was open for 0% of the time, Pallas kernels for 0%

profile of v5, /device:TPU:1, one launch (start us, length us, event | category | flops | bytes accessed | tf_op | source)
XLA Modules:
  0.0 122.3 jit_solution(10986477775972238685)
XLA Ops:
  0.0 0.1 pad_add_fusion.where_ref
  0.1 1.0 copy-done
  1.1 0.7 copy-done.4
  1.7 0.0 copy-done.5
  1.7 0.8 shard_map.64
  2.6 0.7 pad_maximum_fusion
  3.4 31.3 %all-to-all-start = ((bf16[32,5,2,128]{3,2,1,0:T(2,128)(2,1)}), bf16[32,5,2,128]{3,2,1,0:T(2,128)(2,1)S(1)}, u32[]{:S(2)}, u32[]{:S(2)}) async-start(bf16[32,5,2,128]{3,2,1,0:T(2,128)(2,1)} %pad_maximum_fusion), calls=%async_computation | async-start | bytes 163840 | tf_op jit(solution)/shard_map/all_to_all | solution.py:165
  34.7 3.1 %collective-permute-start = (bf16[192,2048]{1,0:T(8,128)(2,1)}, bf16[192,2048]{1,0:T(8,128)(2,1)S(1)}, u32[]{:S(2)}, u32[]{:S(2)}) collective-permute-start(bf16[192,2048]{1,0:T(8,128)(2,1)} %bitcast.21), channel_id=1, source_target_pairs={{0,4},{4,0},{1,5},{5,1},{2,6},{6,2},{3,7},{7,3},{8,12},{12,8},{9,1... | collective-permute-start | bytes 2359304 | tf_op jit(solution)/shard_map/ppermute | solution.py:146
  37.9 1.9 %collective-permute-start.1 = (bf16[192,2048]{1,0:T(8,128)(2,1)}, bf16[192,2048]{1,0:T(8,128)(2,1)S(1)}, u32[]{:S(2)}, u32[]{:S(2)}) collective-permute-start(bf16[192,2048]{1,0:T(8,128)(2,1)} %bitcast.23), channel_id=1, source_target_pairs={{0,4},{4,0},{1,5},{5,1},{2,6},{6,2},{3,7},{7,3},{8,12},{12,8},{9,1... | collective-permute-start | bytes 2359304 | tf_op jit(solution)/shard_map/ppermute | solution.py:146
  39.8 2.4 %collective-permute-start.2 = (bf16[192,2048]{1,0:T(8,128)(2,1)}, bf16[192,2048]{1,0:T(8,128)(2,1)S(1)}, u32[]{:S(2)}, u32[]{:S(2)}) collective-permute-start(bf16[192,2048]{1,0:T(8,128)(2,1)} %bitcast.25), channel_id=1, source_target_pairs={{0,4},{4,0},{1,5},{5,1},{2,6},{6,2},{3,7},{7,3},{8,12},{12,8},{9,1... | collective-permute-start | bytes 2359304 | tf_op jit(solution)/shard_map/ppermute | solution.py:146
  42.2 4.7 %all-to-all-done = bf16[32,5,2,128]{3,2,1,0:T(2,128)(2,1)S(1)} async-done(((bf16[32,5,2,128]{3,2,1,0:T(2,128)(2,1)}), bf16[32,5,2,128]{3,2,1,0:T(2,128)(2,1)S(1)}, u32[]{:S(2)}, u32[]{:S(2)}) %all-to-all-start) | async-done | bytes 81952 | tf_op jit(solution)/shard_map/all_to_all | solution.py:165
  47.0 0.0 copy-start.3
  47.0 0.2 shard_map.65
  47.2 0.0 copy-start.1
  47.2 0.0 copy-start.2
  47.3 0.0 collective-permute-done.gate1
  47.3 0.0 collective-permute-done.1.up1
  47.3 0.0 collective-permute-done.2.down1
  47.3 22.2 %all_to_all.20.x_ref = bf16[16,256,128]{2,1,0:T(8,128)(2,1)S(1)} all-to-all(bf16[16,256,128]{2,1,0:T(8,128)(2,1)S(1)} %shard_map.65), channel_id=1, replica_groups=mesh['node'=32,'x'=4,'core'=2,'cuts'=4] {'cuts','x'}, dimensions={0} | all-to-all | bytes 2097152 | tf_op jit(solution)/shard_map/all_to_all | solution.py:174
  69.5 2.0 %shard_map.66 = bf16[32,128,128]{2,1,0:T(8,128)(2,1)S(1)} custom-call(bf16[16,256,128]{2,1,0:T(8,128)(2,1)S(1)} %all_to_all.20.x_ref, f32[32,128]{1,0:T(8,128)S(1)} %add_bitcast_fusion.scale_ref, bf16[192,2048]{1,0:T(8,128)(2,1)S(1)} %bitcast.22, bf16[192,2048]{1,0:T(8,128)(2,1)S(1)} %bitcast.24, bf16[192,2048]{1,0:T(8,128)(2,1)S(1)} %bitcast.26, ...), custom_call_target="tpu_custom_call" | custom-call | tf_op jit(solution)/shard_map/pallas_call | solution.py:129
  71.5 22.0 %all_to_all.21.in_ref = bf16[32,128,128]{2,1,0:T(8,128)(2,1)S(1)} all-to-all(bf16[32,128,128]{2,1,0:T(8,128)(2,1)S(1)} %shard_map.66), channel_id=1, replica_groups=mesh['node'=32,'x'=4,'core'=2,'cuts'=4] {'x','core','cuts'}, dimensions={0} | all-to-all | bytes 2097152 | tf_op jit(solution)/shard_map/all_to_all | solution.py:177
  93.4 0.2 shard_map.67
  93.6 27.8 %all_to_all.22 = bf16[32,8,128]{2,1,0:T(8,128)(2,1)S(1)} all-to-all(bf16[32,8,128]{2,1,0:T(8,128)(2,1)S(1)} %bitcast.27), channel_id=1, replica_groups={{512,544,576,608,640,672,704,736,768,800,832,864,896,928,960,992,0,32,6..., dimensions={0} | all-to-all | bytes 131072 | tf_op jit(solution)/shard_map/all_to_all | solution.py:179
  121.5 0.8 shard_map.68
  (11 shorter events, 0.1 us)
Async XLA Ops:
  0.0 1.0 copy-start
  1.0 0.7 copy-start.4
  1.0 0.7 copy-start.5
  3.4 43.5 %all-to-all-start = ((bf16[32,5,2,128]{3,2,1,0:T(2,128)(2,1)}), bf16[32,5,2,128]{3,2,1,0:T(2,128)(2,1)S(1)}, u32[]{:S(2)}, u32[]{:S(2)}) async-start(bf16[32,5,2,128]{3,2,1,0:T(2,128)(2,1)} %pad_maximum_fusion), calls=%async_computation | async-start | bytes 163840 | tf_op jit(solution)/shard_map/all_to_all | solution.py:165
  34.7 12.5 %collective-permute-start = (bf16[192,2048]{1,0:T(8,128)(2,1)}, bf16[192,2048]{1,0:T(8,128)(2,1)S(1)}, u32[]{:S(2)}, u32[]{:S(2)}) collective-permute-start(bf16[192,2048]{1,0:T(8,128)(2,1)} %bitcast.21), channel_id=1, source_target_pairs={{0,4},{4,0},{1,5},{5,1},{2,6},{6,2},{3,7},{7,3},{8,12},{12,8},{9,1... | collective-permute-start | bytes 2359304 | tf_op jit(solution)/shard_map/ppermute | solution.py:146
  37.9 9.4 %collective-permute-start.1 = (bf16[192,2048]{1,0:T(8,128)(2,1)}, bf16[192,2048]{1,0:T(8,128)(2,1)S(1)}, u32[]{:S(2)}, u32[]{:S(2)}) collective-permute-start(bf16[192,2048]{1,0:T(8,128)(2,1)} %bitcast.23), channel_id=1, source_target_pairs={{0,4},{4,0},{1,5},{5,1},{2,6},{6,2},{3,7},{7,3},{8,12},{12,8},{9,1... | collective-permute-start | bytes 2359304 | tf_op jit(solution)/shard_map/ppermute | solution.py:146
  39.8 7.5 %collective-permute-start.2 = (bf16[192,2048]{1,0:T(8,128)(2,1)}, bf16[192,2048]{1,0:T(8,128)(2,1)S(1)}, u32[]{:S(2)}, u32[]{:S(2)}) collective-permute-start(bf16[192,2048]{1,0:T(8,128)(2,1)} %bitcast.25), channel_id=1, source_target_pairs={{0,4},{4,0},{1,5},{5,1},{2,6},{6,2},{3,7},{7,3},{8,12},{12,8},{9,1... | collective-permute-start | bytes 2359304 | tf_op jit(solution)/shard_map/ppermute | solution.py:146
  47.0 22.5 %copy-start.3 = (bf16[1,192,2048]{2,1,0:T(8,128)(2,1)S(1)}, bf16[1,192,2048]{2,1,0:T(8,128)(2,1)}, u32[]{:S(2)}) copy-start(bf16[1,192,2048]{2,1,0:T(8,128)(2,1)} %param.11) | copy-start | bytes 2359300
  47.2 22.2 %copy-start.1 = (bf16[1,2048,192]{1,2,0:T(8,128)(2,1)S(1)}, bf16[1,2048,192]{1,2,0:T(8,128)(2,1)}, u32[]{:S(2)}) copy-start(bf16[1,2048,192]{1,2,0:T(8,128)(2,1)} %param.9) | copy-start | bytes 2359300
  47.2 22.2 %copy-start.2 = (bf16[1,2048,192]{1,2,0:T(8,128)(2,1)S(1)}, bf16[1,2048,192]{1,2,0:T(8,128)(2,1)}, u32[]{:S(2)}) copy-start(bf16[1,2048,192]{1,2,0:T(8,128)(2,1)} %param.10) | copy-start | bytes 2359300

commit v6 on v5

--- a/solution.py
+++ b/solution.py
@@ -25,10 +25,10 @@
 PARAMS = pltpu.CompilerParams(vmem_limit_bytes=16 * 1024 * 1024)
 
 
-def seat_kernel(where_ref, ids_ref, route_ref, tok_ref, out_ref, scale_ref, pos_ref):
+def seat_kernel(where_ref, ids_ref, route_ref, out_ref, scale_ref, pos_ref):
     core = where_ref[0]
     column = where_ref[1]
-    tokens = tok_ref.shape[0]
+    tokens = ids_ref.shape[1]
     groups = (lax.broadcasted_iota(jnp.int32, (NODES, tokens), 0) + FIRST) & (NODES - 1)
     named = jnp.zeros((NODES, tokens), F32)
     weight = jnp.zeros((NODES, tokens), F32)
@@ -46,14 +46,18 @@
     seat = lax.broadcasted_iota(jnp.int32, (1, HALF, 1), 1)
     seated = pos[:, None, :] == (seat + core * HALF).astype(F32)
     rows = jnp.where(seated, 1.0, 0.0).reshape(ROWS, tokens).astype(BF16)
-    picked = jnp.dot(rows, tok_ref[...], preferred_element_type=F32)
-    out_ref[...] = picked.reshape(NODES, HALF, LANES).astype(BF16)
+    out_ref[...] = rows
     scale = jnp.sum(jnp.where(seated, weight[:, None, :], 0.0), axis=2, keepdims=True)
     lane = lax.broadcasted_iota(jnp.int32, (1, 1, LANES), 2)
     scale = jnp.sum(jnp.where(lane == seat, scale, 0.0), axis=1)
     high = scale.astype(BF16)
     scale_ref[0] = high
     scale_ref[1] = (scale - high.astype(F32)).astype(BF16)
+
+
+def pick_kernel(rows_ref, tok_ref, out_ref):
+    picked = jnp.dot(rows_ref[...], tok_ref[...], preferred_element_type=F32)
+    out_ref[...] = picked.reshape(NODES, HALF, LANES).astype(BF16)
 
 
 def copies_kernel(in_ref, out_ref):
@@ -150,16 +154,16 @@
     seats, scale, pos = call(
         seat_kernel,
         [
-            ((NODES, HALF, LANES), BF16),
+            ((ROWS, tokens.shape[0]), BF16),
             ((2, NODES, LANES), BF16),
             ((NODES, tokens.shape[0]), F32),
         ],
         where,
         expert_ids.T,
         route_weight.T,
-        block,
-        specs=[SMEM, VMEM, VMEM, VMEM],
-    )
+        specs=[SMEM, VMEM, VMEM],
+    )
+    seats = call(pick_kernel, [((NODES, HALF, LANES), BF16)], seats, block)
     scale = jnp.swapaxes(scale, 0, 1).reshape(NODES, 1, 2, LANES)
     seats = jnp.concatenate([seats.reshape(NODES, 4, 2, LANES), scale], axis=1)
     seats = exchange(seats, "node", axis_index_groups=out_ring)

time: 123 us -> 122 us (level)
    pallas_call x5 -> x6, Pallas kernels: 4.09 us -> 4.22 us  [call(): pl.pallas_call(kernel, out_shape=shapes if many else shapes[0], in_specs=...]
where the time goes in v6:
time: 122 us; the launch traced here: 121 us
  blocking collectives  71.9 us (59%)
  starting transfers between devices  38.8 us (32%)
  waiting for transfers between devices  4.7 us (4%)
  Pallas kernels  4.22 us (3%)
    all_to_all x1, starting transfers between devices, per_device(): seats = exchange(seats, 'node', axis_index_groups=out_ring)  31.3 us
    all_to_all x1, blocking collectives, per_device(): exchange(total.reshape(NODES, HALF, LANES), 'node', axis_index_groups=bac...  27.8 us
    all_to_all x1, blocking collectives, per_device(): rows = exchange(copies, ('cuts', 'x'))  22.2 us
    all_to_all x1, blocking collectives, per_device(): parts = exchange(parts, plane)  22 us
    ppermute x3, starting transfers between devices, per_device(): weights = weights + tuple((lax.ppermute(w, 'core', pairs) for w in weights))  7.48 us
    all_to_all x1, waiting for transfers between devices, per_device(): seats = exchange(seats, 'node', axis_index_groups=out_ring)  4.69 us
    pallas_call x6, Pallas kernels, call(): pl.pallas_call(kernel, out_shape=shapes if many else shapes[0], in_specs=...  4.22 us
  transfers between devices with their start and end apart: 4, of which 1 were waited for; matrix products, arithmetic and copies ran while one was open for 0% of the time, Pallas kernels for 0%

profile of v6, /device:TPU:1, one launch (start us, length us, event | category | flops | bytes accessed | tf_op | source)
XLA Modules:
  0.0 121.5 jit_solution(14679114523736345822)
XLA Ops:
  0.0 0.1 pad_add_fusion.where_ref
  0.1 0.7 copy-done.5
  0.7 0.0 copy-done.4
  0.8 0.8 shard_map.64
  1.7 0.1 shard_map.65
  1.8 0.7 pad_maximum_fusion
  2.6 31.3 %all-to-all-start = ((bf16[32,5,2,128]{3,2,1,0:T(2,128)(2,1)}), bf16[32,5,2,128]{3,2,1,0:T(2,128)(2,1)S(1)}, u32[]{:S(2)}, u32[]{:S(2)}) async-start(bf16[32,5,2,128]{3,2,1,0:T(2,128)(2,1)} %pad_maximum_fusion), calls=%async_computation | async-start | bytes 163840 | tf_op jit(solution)/shard_map/all_to_all | solution.py:169
  33.9 3.1 %collective-permute-start = (bf16[192,2048]{1,0:T(8,128)(2,1)}, bf16[192,2048]{1,0:T(8,128)(2,1)S(1)}, u32[]{:S(2)}, u32[]{:S(2)}) collective-permute-start(bf16[192,2048]{1,0:T(8,128)(2,1)} %bitcast.21), channel_id=1, source_target_pairs={{0,4},{4,0},{1,5},{5,1},{2,6},{6,2},{3,7},{7,3},{8,12},{12,8},{9,1... | collective-permute-start | bytes 2359304 | tf_op jit(solution)/shard_map/ppermute | solution.py:150
  37.1 1.9 %collective-permute-start.1 = (bf16[192,2048]{1,0:T(8,128)(2,1)}, bf16[192,2048]{1,0:T(8,128)(2,1)S(1)}, u32[]{:S(2)}, u32[]{:S(2)}) collective-permute-start(bf16[192,2048]{1,0:T(8,128)(2,1)} %bitcast.23), channel_id=1, source_target_pairs={{0,4},{4,0},{1,5},{5,1},{2,6},{6,2},{3,7},{7,3},{8,12},{12,8},{9,1... | collective-permute-start | bytes 2359304 | tf_op jit(solution)/shard_map/ppermute | solution.py:150
  39.0 2.4 %collective-permute-start.2 = (bf16[192,2048]{1,0:T(8,128)(2,1)}, bf16[192,2048]{1,0:T(8,128)(2,1)S(1)}, u32[]{:S(2)}, u32[]{:S(2)}) collective-permute-start(bf16[192,2048]{1,0:T(8,128)(2,1)} %bitcast.25), channel_id=1, source_target_pairs={{0,4},{4,0},{1,5},{5,1},{2,6},{6,2},{3,7},{7,3},{8,12},{12,8},{9,1... | collective-permute-start | bytes 2359304 | tf_op jit(solution)/shard_map/ppermute | solution.py:150
  41.4 4.7 %all-to-all-done = bf16[32,5,2,128]{3,2,1,0:T(2,128)(2,1)S(1)} async-done(((bf16[32,5,2,128]{3,2,1,0:T(2,128)(2,1)}), bf16[32,5,2,128]{3,2,1,0:T(2,128)(2,1)S(1)}, u32[]{:S(2)}, u32[]{:S(2)}) %all-to-all-start) | async-done | bytes 81952 | tf_op jit(solution)/shard_map/all_to_all | solution.py:169
  46.2 0.0 copy-start.3
  46.2 0.2 shard_map.66
  46.4 0.0 copy-start.1
  46.4 0.0 copy-start.2
  46.5 0.0 collective-permute-done.gate1
  46.5 0.0 collective-permute-done.1.up1
  46.5 0.0 collective-permute-done.2.down1
  46.5 22.2 %all_to_all.20.x_ref = bf16[16,256,128]{2,1,0:T(8,128)(2,1)S(1)} all-to-all(bf16[16,256,128]{2,1,0:T(8,128)(2,1)S(1)} %shard_map.66), channel_id=1, replica_groups=mesh['node'=32,'x'=4,'core'=2,'cuts'=4] {'cuts','x'}, dimensions={0} | all-to-all | bytes 2097152 | tf_op jit(solution)/shard_map/all_to_all | solution.py:178
  68.7 2.0 %shard_map.67 = bf16[32,128,128]{2,1,0:T(8,128)(2,1)S(1)} custom-call(bf16[16,256,128]{2,1,0:T(8,128)(2,1)S(1)} %all_to_all.20.x_ref, f32[32,128]{1,0:T(8,128)S(1)} %add_bitcast_fusion.scale_ref, bf16[192,2048]{1,0:T(8,128)(2,1)S(1)} %bitcast.22, bf16[192,2048]{1,0:T(8,128)(2,1)S(1)} %bitcast.24, bf16[192,2048]{1,0:T(8,128)(2,1)S(1)} %bitcast.26, ...), custom_call_target="tpu_custom_call" | custom-call | tf_op jit(solution)/shard_map/pallas_call | solution.py:133
  70.7 22.0 %all_to_all.21.in_ref = bf16[32,128,128]{2,1,0:T(8,128)(2,1)S(1)} all-to-all(bf16[32,128,128]{2,1,0:T(8,128)(2,1)S(1)} %shard_map.67), channel_id=1, replica_groups=mesh['node'=32,'x'=4,'core'=2,'cuts'=4] {'x','core','cuts'}, dimensions={0} | all-to-all | bytes 2097152 | tf_op jit(solution)/shard_map/all_to_all | solution.py:181
  92.6 0.2 shard_map.68
  92.8 27.8 %all_to_all.22 = bf16[32,8,128]{2,1,0:T(8,128)(2,1)S(1)} all-to-all(bf16[32,8,128]{2,1,0:T(8,128)(2,1)S(1)} %bitcast.27), channel_id=1, replica_groups={{512,544,576,608,640,672,704,736,768,800,832,864,896,928,960,992,0,32,6..., dimensions={0} | all-to-all | bytes 131072 | tf_op jit(solution)/shard_map/all_to_all | solution.py:183
  120.6 0.8 shard_map.69
  (12 shorter events, 0.1 us)
Async XLA Ops:
  0.0 1.6 %copy-start = (bf16[128,2048]{1,0:T(8,128)(2,1)S(1)}, bf16[128,2048]{1,0:T(8,128)(2,1)}, u32[]{:S(2)}) copy-start(bf16[128,2048]{1,0:T(8,128)(2,1)} %param.6) | copy-start | bytes 1572868
  0.0 0.7 copy-start.5
  0.0 0.8 copy-start.4
  2.6 43.6 %all-to-all-start = ((bf16[32,5,2,128]{3,2,1,0:T(2,128)(2,1)}), bf16[32,5,2,128]{3,2,1,0:T(2,128)(2,1)S(1)}, u32[]{:S(2)}, u32[]{:S(2)}) async-start(bf16[32,5,2,128]{3,2,1,0:T(2,128)(2,1)} %pad_maximum_fusion), calls=%async_computation | async-start | bytes 163840 | tf_op jit(solution)/shard_map/all_to_all | solution.py:169
  33.9 12.5 %collective-permute-start = (bf16[192,2048]{1,0:T(8,128)(2,1)}, bf16[192,2048]{1,0:T(8,128)(2,1)S(1)}, u32[]{:S(2)}, u32[]{:S(2)}) collective-permute-start(bf16[192,2048]{1,0:T(8,128)(2,1)} %bitcast.21), channel_id=1, source_target_pairs={{0,4},{4,0},{1,5},{5,1},{2,6},{6,2},{3,7},{7,3},{8,12},{12,8},{9,1... | collective-permute-start | bytes 2359304 | tf_op jit(solution)/shard_map/ppermute | solution.py:150
  37.1 9.4 %collective-permute-start.1 = (bf16[192,2048]{1,0:T(8,128)(2,1)}, bf16[192,2048]{1,0:T(8,128)(2,1)S(1)}, u32[]{:S(2)}, u32[]{:S(2)}) collective-permute-start(bf16[192,2048]{1,0:T(8,128)(2,1)} %bitcast.23), channel_id=1, source_target_pairs={{0,4},{4,0},{1,5},{5,1},{2,6},{6,2},{3,7},{7,3},{8,12},{12,8},{9,1... | collective-permute-start | bytes 2359304 | tf_op jit(solution)/shard_map/ppermute | solution.py:150
  39.0 7.5 %collective-permute-start.2 = (bf16[192,2048]{1,0:T(8,128)(2,1)}, bf16[192,2048]{1,0:T(8,128)(2,1)S(1)}, u32[]{:S(2)}, u32[]{:S(2)}) collective-permute-start(bf16[192,2048]{1,0:T(8,128)(2,1)} %bitcast.25), channel_id=1, source_target_pairs={{0,4},{4,0},{1,5},{5,1},{2,6},{6,2},{3,7},{7,3},{8,12},{12,8},{9,1... | collective-permute-start | bytes 2359304 | tf_op jit(solution)/shard_map/ppermute | solution.py:150
  46.2 22.5 %copy-start.3 = (bf16[1,192,2048]{2,1,0:T(8,128)(2,1)S(1)}, bf16[1,192,2048]{2,1,0:T(8,128)(2,1)}, u32[]{:S(2)}) copy-start(bf16[1,192,2048]{2,1,0:T(8,128)(2,1)} %param.11) | copy-start | bytes 2359300
  46.4 22.2 %copy-start.1 = (bf16[1,2048,192]{1,2,0:T(8,128)(2,1)S(1)}, bf16[1,2048,192]{1,2,0:T(8,128)(2,1)}, u32[]{:S(2)}) copy-start(bf16[1,2048,192]{1,2,0:T(8,128)(2,1)} %param.9) | copy-start | bytes 2359300
  46.4 22.2 %copy-start.2 = (bf16[1,2048,192]{1,2,0:T(8,128)(2,1)S(1)}, bf16[1,2048,192]{1,2,0:T(8,128)(2,1)}, u32[]{:S(2)}) copy-start(bf16[1,2048,192]{1,2,0:T(8,128)(2,1)} %param.10) | copy-start | bytes 2359300

commit v7 on v6

--- a/solution.py
+++ b/solution.py
@@ -10,7 +10,7 @@
 F32 = jnp.float32
 BF16 = jnp.bfloat16
 NODES = 32
-FIRST = 20
+FIRST = 18
 BACK = 16
 TURN = FIRST - BACK
 CHIPS = 16

time: 122 us -> 122 us (level)
  starting transfers between devices: 38.8 us -> 41.8 us
  waiting for transfers between devices: 4.7 us -> 2.06 us
    all_to_all x1, starting transfers between devices: 31.3 us -> 34.4 us  [per_device(): seats = exchange(seats, 'node', axis_index_groups=out_ring)]
    all_to_all x1, waiting for transfers between devices: 4.69 us -> 2.06 us  [per_device(): seats = exchange(seats, 'node', axis_index_groups=out_ring)]
where the time goes in v7:
time: 122 us
  blocking collectives  71.7 us (59%)
  starting transfers between devices  41.8 us (34%)
  Pallas kernels  4.22 us (3%)
  waiting for transfers between devices  2.06 us (2%)
    all_to_all x1, starting transfers between devices, per_device(): seats = exchange(seats, 'node', axis_index_groups=out_ring)  34.4 us
    all_to_all x1, blocking collectives, per_device(): exchange(total.reshape(NODES, HALF, LANES), 'node', axis_index_groups=bac...  27.6 us
    all_to_all x1, blocking collectives, per_device(): rows = exchange(copies, ('cuts', 'x'))  22.6 us
    all_to_all x1, blocking collectives, per_device(): parts = exchange(parts, plane)  21.5 us
    ppermute x3, starting transfers between devices, per_device(): weights = weights + tuple((lax.ppermute(w, 'core', pairs) for w in weights))  7.48 us
    pallas_call x6, Pallas kernels, call(): pl.pallas_call(kernel, out_shape=shapes if many else shapes[0], in_specs=...  4.22 us
  transfers between devices with their start and end apart: 4, of which 1 were waited for; matrix products, arithmetic and copies ran while one was open for 0% of the time, Pallas kernels for 0%

profile of v7, /device:TPU:1, one launch (start us, length us, event | category | flops | bytes accessed | tf_op | source)
XLA Modules:
  0.0 121.6 jit_solution(2078090514920335103)
XLA Ops:
  0.0 0.1 pad_add_fusion.where_ref
  0.1 0.7 copy-done.5
  0.7 0.0 copy-done.4
  0.8 0.8 shard_map.64
  1.7 0.1 shard_map.65
  1.8 0.7 pad_maximum_fusion
  2.6 34.4 %all-to-all-start = ((bf16[32,5,2,128]{3,2,1,0:T(2,128)(2,1)}), bf16[32,5,2,128]{3,2,1,0:T(2,128)(2,1)S(1)}, u32[]{:S(2)}, u32[]{:S(2)}) async-start(bf16[32,5,2,128]{3,2,1,0:T(2,128)(2,1)} %pad_maximum_fusion), calls=%async_computation | async-start | bytes 163840 | tf_op jit(solution)/shard_map/all_to_all | solution.py:169
  36.9 3.1 %collective-permute-start = (bf16[192,2048]{1,0:T(8,128)(2,1)}, bf16[192,2048]{1,0:T(8,128)(2,1)S(1)}, u32[]{:S(2)}, u32[]{:S(2)}) collective-permute-start(bf16[192,2048]{1,0:T(8,128)(2,1)} %bitcast.21), channel_id=1, source_target_pairs={{0,4},{4,0},{1,5},{5,1},{2,6},{6,2},{3,7},{7,3},{8,12},{12,8},{9,1... | collective-permute-start | bytes 2359304 | tf_op jit(solution)/shard_map/ppermute | solution.py:150
  40.1 1.9 %collective-permute-start.1 = (bf16[192,2048]{1,0:T(8,128)(2,1)}, bf16[192,2048]{1,0:T(8,128)(2,1)S(1)}, u32[]{:S(2)}, u32[]{:S(2)}) collective-permute-start(bf16[192,2048]{1,0:T(8,128)(2,1)} %bitcast.23), channel_id=1, source_target_pairs={{0,4},{4,0},{1,5},{5,1},{2,6},{6,2},{3,7},{7,3},{8,12},{12,8},{9,1... | collective-permute-start | bytes 2359304 | tf_op jit(solution)/shard_map/ppermute | solution.py:150
  42.0 2.4 %collective-permute-start.2 = (bf16[192,2048]{1,0:T(8,128)(2,1)}, bf16[192,2048]{1,0:T(8,128)(2,1)S(1)}, u32[]{:S(2)}, u32[]{:S(2)}) collective-permute-start(bf16[192,2048]{1,0:T(8,128)(2,1)} %bitcast.25), channel_id=1, source_target_pairs={{0,4},{4,0},{1,5},{5,1},{2,6},{6,2},{3,7},{7,3},{8,12},{12,8},{9,1... | collective-permute-start | bytes 2359304 | tf_op jit(solution)/shard_map/ppermute | solution.py:150
  44.4 2.1 %all-to-all-done = bf16[32,5,2,128]{3,2,1,0:T(2,128)(2,1)S(1)} async-done(((bf16[32,5,2,128]{3,2,1,0:T(2,128)(2,1)}), bf16[32,5,2,128]{3,2,1,0:T(2,128)(2,1)S(1)}, u32[]{:S(2)}, u32[]{:S(2)}) %all-to-all-start) | async-done | bytes 81952 | tf_op jit(solution)/shard_map/all_to_all | solution.py:169
  46.5 0.0 copy-start.3
  46.5 0.2 shard_map.66
  46.8 0.0 copy-start.1
  46.8 0.0 copy-start.2
  46.8 0.0 collective-permute-done.gate1
  46.8 0.0 collective-permute-done.1.up1
  46.8 0.0 collective-permute-done.2.down1
  46.9 22.6 %all_to_all.20.x_ref = bf16[16,256,128]{2,1,0:T(8,128)(2,1)S(1)} all-to-all(bf16[16,256,128]{2,1,0:T(8,128)(2,1)S(1)} %shard_map.66), channel_id=1, replica_groups=mesh['node'=32,'x'=4,'core'=2,'cuts'=4] {'cuts','x'}, dimensions={0} | all-to-all | bytes 2097152 | tf_op jit(solution)/shard_map/all_to_all | solution.py:178
  69.5 2.0 %shard_map.67 = bf16[32,128,128]{2,1,0:T(8,128)(2,1)S(1)} custom-call(bf16[16,256,128]{2,1,0:T(8,128)(2,1)S(1)} %all_to_all.20.x_ref, f32[32,128]{1,0:T(8,128)S(1)} %add_bitcast_fusion.scale_ref, bf16[192,2048]{1,0:T(8,128)(2,1)S(1)} %bitcast.22, bf16[192,2048]{1,0:T(8,128)(2,1)S(1)} %bitcast.24, bf16[192,2048]{1,0:T(8,128)(2,1)S(1)} %bitcast.26, ...), custom_call_target="tpu_custom_call" | custom-call | tf_op jit(solution)/shard_map/pallas_call | solution.py:133
  71.5 21.5 %all_to_all.21.in_ref = bf16[32,128,128]{2,1,0:T(8,128)(2,1)S(1)} all-to-all(bf16[32,128,128]{2,1,0:T(8,128)(2,1)S(1)} %shard_map.67), channel_id=1, replica_groups=mesh['node'=32,'x'=4,'core'=2,'cuts'=4] {'x','core','cuts'}, dimensions={0} | all-to-all | bytes 2097152 | tf_op jit(solution)/shard_map/all_to_all | solution.py:181
  93.0 0.2 shard_map.68
  93.2 27.6 %all_to_all.22 = bf16[32,8,128]{2,1,0:T(8,128)(2,1)S(1)} all-to-all(bf16[32,8,128]{2,1,0:T(8,128)(2,1)S(1)} %bitcast.27), channel_id=1, replica_groups={{512,544,576,608,640,672,704,736,768,800,832,864,896,928,960,992,0,32,6..., dimensions={0} | all-to-all | bytes 131072 | tf_op jit(solution)/shard_map/all_to_all | solution.py:183
  120.8 0.8 shard_map.69
  (12 shorter events, 0.1 us)
Async XLA Ops:
  0.0 1.6 %copy-start = (bf16[128,2048]{1,0:T(8,128)(2,1)S(1)}, bf16[128,2048]{1,0:T(8,128)(2,1)}, u32[]{:S(2)}) copy-start(bf16[128,2048]{1,0:T(8,128)(2,1)} %param.6) | copy-start | bytes 1572868
  0.0 0.7 copy-start.5
  0.0 0.8 copy-start.4
  2.6 43.9 %all-to-all-start = ((bf16[32,5,2,128]{3,2,1,0:T(2,128)(2,1)}), bf16[32,5,2,128]{3,2,1,0:T(2,128)(2,1)S(1)}, u32[]{:S(2)}, u32[]{:S(2)}) async-start(bf16[32,5,2,128]{3,2,1,0:T(2,128)(2,1)} %pad_maximum_fusion), calls=%async_computation | async-start | bytes 163840 | tf_op jit(solution)/shard_map/all_to_all | solution.py:169
  36.9 9.9 %collective-permute-start = (bf16[192,2048]{1,0:T(8,128)(2,1)}, bf16[192,2048]{1,0:T(8,128)(2,1)S(1)}, u32[]{:S(2)}, u32[]{:S(2)}) collective-permute-start(bf16[192,2048]{1,0:T(8,128)(2,1)} %bitcast.21), channel_id=1, source_target_pairs={{0,4},{4,0},{1,5},{5,1},{2,6},{6,2},{3,7},{7,3},{8,12},{12,8},{9,1... | collective-permute-start | bytes 2359304 | tf_op jit(solution)/shard_map/ppermute | solution.py:150
  40.1 6.8 %collective-permute-start.1 = (bf16[192,2048]{1,0:T(8,128)(2,1)}, bf16[192,2048]{1,0:T(8,128)(2,1)S(1)}, u32[]{:S(2)}, u32[]{:S(2)}) collective-permute-start(bf16[192,2048]{1,0:T(8,128)(2,1)} %bitcast.23), channel_id=1, source_target_pairs={{0,4},{4,0},{1,5},{5,1},{2,6},{6,2},{3,7},{7,3},{8,12},{12,8},{9,1... | collective-permute-start | bytes 2359304 | tf_op jit(solution)/shard_map/ppermute | solution.py:150
  42.0 4.8 %collective-permute-start.2 = (bf16[192,2048]{1,0:T(8,128)(2,1)}, bf16[192,2048]{1,0:T(8,128)(2,1)S(1)}, u32[]{:S(2)}, u32[]{:S(2)}) collective-permute-start(bf16[192,2048]{1,0:T(8,128)(2,1)} %bitcast.25), channel_id=1, source_target_pairs={{0,4},{4,0},{1,5},{5,1},{2,6},{6,2},{3,7},{7,3},{8,12},{12,8},{9,1... | collective-permute-start | bytes 2359304 | tf_op jit(solution)/shard_map/ppermute | solution.py:150
  46.5 22.9 %copy-start.3 = (bf16[1,192,2048]{2,1,0:T(8,128)(2,1)S(1)}, bf16[1,192,2048]{2,1,0:T(8,128)(2,1)}, u32[]{:S(2)}) copy-start(bf16[1,192,2048]{2,1,0:T(8,128)(2,1)} %param.11) | copy-start | bytes 2359300
  46.8 22.7 %copy-start.1 = (bf16[1,2048,192]{1,2,0:T(8,128)(2,1)S(1)}, bf16[1,2048,192]{1,2,0:T(8,128)(2,1)}, u32[]{:S(2)}) copy-start(bf16[1,2048,192]{1,2,0:T(8,128)(2,1)} %param.9) | copy-start | bytes 2359300
  46.8 22.7 %copy-start.2 = (bf16[1,2048,192]{1,2,0:T(8,128)(2,1)S(1)}, bf16[1,2048,192]{1,2,0:T(8,128)(2,1)}, u32[]{:S(2)}) copy-start(bf16[1,2048,192]{1,2,0:T(8,128)(2,1)} %param.10) | copy-start | bytes 2359300
